TPU v7x, 128 devices: a whole 4x4x4 slice. The times are simulated.
128 devices in a mesh: dp: 64 (over y, x, z_hi, core), tensor: 2 (over z_lo).
Axes of the slice: x: 4, y: 4, z: 4 (z_hi: 2, z_lo: 2; z = z_hi * 2 + z_lo), core: 2. Of those that a mesh axis runs over, the one named last changes fastest.
Arguments:
- tokens: bfloat16 [32768, 1024], P(('dp', 'tensor')), may hold values from -6 to 6
- segment: int32 [32768], P('dp'), may hold values from -1 to 255, as said below
- w_query: bfloat16 [1024, 1024], P('dp', 'tensor'), may hold values from -0.1875 to 0.1875
- w_key: bfloat16 [1024, 1024], P('dp', 'tensor'), may hold values from -0.1875 to 0.1875
- w_value: bfloat16 [1024, 1024], P('dp', 'tensor'), may hold values from -0.1875 to 0.1875
- w_out: bfloat16 [1024, 1024], P('dp', 'tensor'), may hold values from -0.75 to 0.75
- w_up: bfloat16 [1024, 4096], P('dp', 'tensor'), may hold values from -0.1875 to 0.1875
- w_down: bfloat16 [1024, 4096], P('dp', 'tensor'), may hold values from -0.09375 to 0.09375
- b_query: bfloat16 [1024], P(('tensor', 'dp')), may hold values from -3 to 3
- b_value: bfloat16 [1024], P(('tensor', 'dp')), may hold values from -3 to 3
- b_up: bfloat16 [4096], P(('tensor', 'dp')), may hold values from -3 to 3
- b_out: bfloat16 [1024], P('dp'), may hold values from -3 to 3
- b_down: bfloat16 [1024], P('dp'), may hold values from -3 to 3
- gain_one: bfloat16 [1024], P('dp'), may hold values from 0.5 to 1.5
- shift_one: bfloat16 [1024], P('dp'), may hold values from -3 to 3
- gain_two: bfloat16 [1024], P('dp'), may hold values from 0.5 to 1.5
- shift_two: bfloat16 [1024], P('dp'), may hold values from -3 to 3
- out_grad: float32 [32768, 1024], P(('dp', 'tensor')), may hold values from -6 to 6
Outputs:
- layer_out: bfloat16 [32768, 1024], P(('dp', 'tensor'))
- input_grad: float32 [32768, 1024], P(('dp', 'tensor'))
- grad_w_query: float32 [1024, 1024], P('dp', 'tensor')
- grad_w_key: float32 [1024, 1024], P('dp', 'tensor')
- grad_w_value: float32 [1024, 1024], P('dp', 'tensor')
- grad_w_out: float32 [1024, 1024], P('dp', 'tensor')
- grad_w_up: float32 [1024, 4096], P('dp', 'tensor')
- grad_w_down: float32 [1024, 4096], P('dp', 'tensor')
- grad_b_query: float32 [1024], P(('tensor', 'dp'))
- grad_b_value: float32 [1024], P(('tensor', 'dp'))
- grad_b_up: float32 [4096], P(('tensor', 'dp'))
- grad_b_out: float32 [1024], P('dp')
- grad_b_down: float32 [1024], P('dp')
- grad_gain_one: float32 [1024], P('dp')
- grad_shift_one: float32 [1024], P('dp')
- grad_gain_two: float32 [1024], P('dp')
- grad_shift_two: float32 [1024], P('dp')
Inputs may be any that keep to these rules, and one draw needn't show every extreme that they name: `segment`: within each group of 512 slots the live slots come first and carry sequence numbers 0, 1, 2, ... in order, each sequence in consecutive slots; the slots after them hold -1. Sequence 0 of every group covers more than half of its slots. At least one group has no padding, and in it the last slot carries the largest sequence number.
All inputs are finite; a program needn't handle non-finite values.
Results may differ from a plain program's by a relative error of at most 0.015.
Values may be sent and summed in bfloat16 or wider, within the bound.
A program may use at most 128 MiB of HBM per device.

v0:
```python
import functools

import jax
import jax.numpy as jnp
from jax import lax
from jax.experimental import pallas as pl
from jax.experimental.pallas import tpu as pltpu
from jax.sharding import PartitionSpec as P

MESH = pl.DeviceIdType.MESH
F32 = jnp.float32
BF16 = jnp.bfloat16

SQUARES = ((1, "a"), (0, "a"), (2, "a"), (1, "b"), (0, "b"), (2, "b"))
TILES = 24
COLS = 256
ROUTES = 6
VEC_ROWS = 96


def position():
    dp, low = lax.axis_index("dp"), lax.axis_index("tensor")
    return (dp // 16, lax.rem(dp // 4, 4), lax.rem(dp // 2, 2) * 2 + low), lax.rem(dp, 2)


def device(chip, core):
    y, x, z = chip
    return (y * 16 + x * 4 + (z // 2) * 2 + core, lax.rem(z, 2))


def across(chip, square):
    axis, kind = square
    at = chip[axis]
    new = at + 1 - 2 * lax.rem(at, 2) if kind == "a" else 3 - at
    return tuple(new if k == axis else c for k, c in enumerate(chip))


def route_squares(route):
    return [SQUARES[(route + s) % 6] for s in range(6)]


def pieces(chip, done):
    per_axis = []
    for axis in range(3):
        at = chip[axis]
        kinds = {kind for a, kind in done if a == axis}
        if not kinds:
            per_axis.append([(at, 1)])
        elif kinds == {"a"}:
            per_axis.append([(at // 2 * 2, 2)])
        elif kinds == {"b"}:
            per_axis.append([(at, 1), (3 - at, 1)])
        else:
            per_axis.append([(0, 4)])
    return [
        ((ky, kx, kz), (y, x, z))
        for ky, y in enumerate(per_axis[0])
        for kx, x in enumerate(per_axis[1])
        for kz, z in enumerate(per_axis[2])
    ]


def span(done):
    sizes = []
    for axis in range(3):
        kinds = {kind for a, kind in done if a == axis}
        sizes.append(1 << len(kinds))
    return sizes


def view(ref, tiles, piece):
    return ref.at[(pl.ds(*tiles),) + tuple(pl.ds(*p) for p in piece)]


def piece_counts():
    return [[len(pieces((0, 0, 0), route_squares(r)[:s])) for s in range(6)] for r in range(ROUTES)]


COUNTS = piece_counts()
COPIES = sum(map(sum, COUNTS))


def first_sem(route, stage):
    return sum(sum(c) for c in COUNTS[:route]) + sum(COUNTS[route][:stage])


class Gather:
    def __init__(self, w, send, recv, tiles_of, base=0):
        self.w, self.send, self.recv, self.tiles_of, self.base = w, send, recv, tiles_of, base
        self.chip, self.core = position()

    def copies(self, route, stage):
        squares = route_squares(route)
        target = device(across(self.chip, squares[stage]), self.core)
        out = []
        for n, (_, piece) in enumerate(pieces(self.chip, squares[:stage])):
            part = view(self.w, self.tiles_of(route), piece)
            sem = self.base + first_sem(route, stage) + n
            out.append(
                pltpu.make_async_remote_copy(
                    src_ref=part,
                    dst_ref=part,
                    send_sem=self.send.at[sem],
                    recv_sem=self.recv.at[sem],
                    device_id=target,
                    device_id_type=MESH,
                )
            )
        return out

    def start(self, route, stage):
        for c in self.copies(route, stage):
            c.start()

    def wait_recv(self, route, stage):
        for c in self.copies(route, stage):
            c.wait_recv()

    def wait_send(self, route, stage):
        for c in self.copies(route, stage):
            c.wait_send()


def landing_shapes(tiles_of):
    shapes = []
    for route in range(ROUTES):
        for stage in range(6):
            done = route_squares(route)[: 5 - stage]
            (_, piece) = pieces((0, 0, 0), done)[0]
            shapes.append(
                (COUNTS[route][5 - stage], tiles_of(route)[1]) + tuple(n for _, n in piece) + (16, COLS)
            )
    return shapes


class Scatter:
    def __init__(self, g, landings, send, recv, tiles_of, base=0):
        self.g, self.landings, self.send, self.recv = g, landings, send, recv
        self.tiles_of, self.base = tiles_of, base
        self.chip, self.core = position()

    def copies(self, route, stage):
        squares = route_squares(route)[: 6 - stage]
        over = across(self.chip, squares[-1])
        target = device(over, self.core)
        out = []
        for n, (_, piece) in enumerate(pieces(over, squares[:-1])):
            sem = self.base + first_sem(route, 5 - stage) + n
            out.append(
                pltpu.make_async_remote_copy(
                    src_ref=view(self.g, self.tiles_of(route), piece),
                    dst_ref=self.landings[route * 6 + stage].at[n],
                    send_sem=self.send.at[sem],
                    recv_sem=self.recv.at[sem],
                    device_id=target,
                    device_id_type=MESH,
                )
            )
        return out

    def start(self, route, stage):
        for c in self.copies(route, stage):
            c.start()

    def wait_send(self, route, stage):
        for c in self.copies(route, stage):
            c.wait_send()

    def take(self, route, stage):
        for c in self.copies(route, stage):
            c.wait_recv()
        tile0, tiles = self.tiles_of(route)
        done = route_squares(route)[: 5 - stage]
        landed = self.landings[route * 6 + stage]
        for n, (_, piece) in enumerate(pieces(self.chip, done)):
            (y0, ny), (x0, nx), (z0, nz) = piece

            def add(i, carry):
                tile, y = i // ny, lax.rem(i, ny)
                at = (tile0 + tile, y0 + y, pl.ds(x0, nx), pl.ds(z0, nz))
                total = self.g[at].astype(F32) + landed[n, tile, y].astype(F32)
                self.g[at] = total.astype(BF16)
                return carry

            lax.fori_loop(0, tiles * ny, add, 0)


def greet(others):
    barrier = pltpu.get_barrier_semaphore()
    for other in others:
        pl.semaphore_signal(barrier, inc=1, device_id=other, device_id_type=MESH)
    pl.semaphore_wait(barrier, len(others))


def neighbours():
    chip, core = position()
    return [device(across(chip, square), core) for square in SQUARES]


def sibling():
    chip, core = position()
    return device(chip, 1 - core)


class VectorSum:
    def __init__(self, kept, came, send, recv, base):
        self.kept, self.came, self.send, self.recv, self.base = kept, came, send, recv, base

    def copy(self, stage):
        target = (neighbours() + [sibling()])[stage]
        return pltpu.make_async_remote_copy(
            src_ref=self.kept.at[stage],
            dst_ref=self.came.at[stage],
            send_sem=self.send.at[self.base + stage],
            recv_sem=self.recv.at[self.base + stage],
            device_id=target,
            device_id_type=MESH,
        )

    def start(self, stage):
        self.copy(stage).start()

    def take(self, stage):
        self.copy(stage).wait_recv()
        self.kept[stage + 1] = self.kept[stage] + self.came[stage]

    def wait_send(self, stage):
        self.copy(stage).wait_send()


def early_tiles(route):
    return (route, 1)


def late_tiles(route):
    return (6 + route * 3, 3)


GROUP = 512
HALF = 256
WIDTH = 1024
HEAD_DIM = 64
PAIR = 2 * HEAD_DIM
SCALE = HEAD_DIM**-0.5
EPSILON = 1e-12
NN = (((1,), (0,)), ((), ()))
NT = (((1,), (1,)), ((), ()))
TN = (((0,), (0,)), ((), ()))
Q_TILE, OUT_TILE, UP_TILE, DOWN_TILE = 0, 6, 8, 16
WEIGHT_TILES = (2, 2, 2, 2, 8, 8)


def dot(a, b, dims=NN):
    return lax.dot_general(a, b, dims, preferred_element_type=F32)


def loop(count, body):
    def step(i, carry):
        body(i)
        return carry

    lax.fori_loop(0, count, step, 0)


def layer_kernel(
    w_q, w_k, w_v, w_o, w_u, w_d, vec, seg, tokens, out_grad,
    layer_out, input_grad, g_q, g_k, g_v, g_o, g_u, g_d, vec_out,
    w, g, x, n1, gd, tr, qkv, probs, bias, ctx, gctx, ds, part, leave, come,
    hat, inv, d_two, cot, act, slope, segments, segcol, features, biases, bias_sums, sums,
    out_rows, own_grads_q, own_grads_k, own_grads_v, own_grads_o, own_grads_u, own_grads_d,
    kept, came, kept_back, came_back,
    gsend, grecv, ssend, srecv, vsend, vrecv, swap_send, swap_recv, sib_send, sib_recv,
    *landings,
):
    chip, core = position()
    y, x_at, z = chip
    low = lax.rem(z, 2)
    opposite_chip = across(chip, (2, "a"))
    diagonal = device(opposite_chip, 1 - core)
    twin = sibling()
    stays = core == low
    own_rows = pl.ds(pl.multiple_of(core * HALF, HALF), HALF)
    other_rows = pl.ds(pl.multiple_of((1 - core) * HALF, HALF), HALF)

    def swap_copies(n, src, dst_here, dst_there):
        away = pltpu.make_async_remote_copy(
            src_ref=src, dst_ref=dst_there, send_sem=swap_send.at[n], recv_sem=swap_recv.at[n],
            device_id=diagonal, device_id_type=MESH,
        )
        return away, pltpu.make_async_copy(src, dst_here, swap_recv.at[n])

    def swap_start(n, src, dst_here, dst_there):
        away, here = swap_copies(n, src, dst_here, dst_there)
        pl.when(stays)(here.start)
        pl.when(jnp.logical_not(stays))(away.start)

    def swap_wait(n, src, dst_here, dst_there):
        away, here = swap_copies(n, src, dst_here, dst_there)
        pl.when(stays)(here.wait)
        pl.when(jnp.logical_not(stays))(away.wait)

    def to_twin(n, src, dst):
        return pltpu.make_async_remote_copy(
            src_ref=src, dst_ref=dst, send_sem=sib_send.at[n], recv_sem=sib_recv.at[n],
            device_id=twin, device_id_type=MESH,
        )

    greet(neighbours() + [twin, diagonal])

    weight_moves = []
    tile = 0
    for ref, count in zip((w_q, w_k, w_v, w_o, w_u, w_d), WEIGHT_TILES):
        for k in range(count):
            weight_moves.append(
                (
                    tile,
                    ref.at[:, pl.ds(k * COLS, COLS)],
                    w.at[tile, y, x_at, z],
                    w.at[(tile,) + opposite_chip],
                )
            )
            tile += 1
    seg_move = (TILES, seg, segments, segments)
    row_move = (TILES + 1, tokens, x.at[own_rows], x.at[other_rows])
    cot_move = (TILES + 2, out_grad, cot, cot)
    for move in weight_moves:
        swap_start(*move)
    swap_start(*row_move)
    swap_start(*seg_move)
    swap_start(*cot_move)
    vectors = VectorSum(kept, came, vsend, vrecv, 0)
    kept[0] = vec[...]
    vectors.start(0)

    early = Gather(w, gsend, grecv, early_tiles)
    late = Gather(w, gsend, grecv, late_tiles, COPIES)
    for stage in range(4):
        if stage == 0:
            for move in weight_moves:
                swap_wait(*move)
        for phase in (early, late):
            for route in range(ROUTES):
                if stage:
                    phase.wait_recv(route, stage - 1)
                phase.start(route, stage)
        vectors.take(stage)
        vectors.start(stage + 1)
    for stage in (4, 5):
        for route in range(ROUTES):
            early.wait_recv(route, stage - 1)
            early.start(route, stage)
        vectors.take(stage)
        vectors.start(stage + 1)
    for route in range(ROUTES):
        late.wait_recv(route, 3)
        late.start(route, 4)

    swap_wait(*row_move)
    rows_copy = to_twin(0, x.at[own_rows], x.at[own_rows])
    rows_copy.start()
    swap_wait(*seg_move)
    across_lanes = jnp.broadcast_to(segments[0:1, :], (128, GROUP))
    segcol[...] = across_lanes.T
    for k in range(4):
        cols = slice(k * 128, k * 128 + 128)
        bias[:, cols] = jnp.where(segcol[...] == segments[0:1, cols], 0.0, -1000000000.0)
    vectors.take(6)
    for n in range(6):
        for k in range(8):
            features[n, :, k * 128 : k * 128 + 128] = kept[7, 48 + n * 8 + k : 49 + n * 8 + k, :]
    for k in range(2):
        for half in range(2):
            lanes = slice(half * 128, half * 128 + 128)
            biases[k, :, lanes] = kept[7, pl.ds(core * 4 + k * 2 + half, 1), :]
            biases[4 + k, :, lanes] = kept[7, pl.ds(8 + core * 4 + k * 2 + half, 1), :]
        biases[2 + k] = jnp.zeros((1, COLS), F32)
    for k in range(8):
        for half in range(2):
            lanes = slice(half * 128, half * 128 + 128)
            biases[6 + k, :, lanes] = kept[7, pl.ds(16 + core * 16 + k * 2 + half, 1), :]
    rows_copy.wait_recv()

    for route in range(ROUTES):
        early.wait_recv(route, 5)

    def weight(tile):
        return w[tile].reshape(WIDTH, COLS)

    def project(t):
        made = (dot(x[...], weight(t)) + biases[t]).astype(BF16)
        qkv[2 * t] = made[:, :128]
        qkv[2 * t + 1] = made[:, 128:]

    loop(6, project)
    low_lanes = lax.broadcasted_iota(jnp.int32, (1, PAIR), 1) < HEAD_DIM

    def only(head, values):
        keep = low_lanes if head == 0 else jnp.logical_not(low_lanes)
        return jnp.where(keep, values, jnp.zeros_like(values))

    def attend(pair):
        for half in range(2):
            rows = slice(half * HALF, half * HALF + HALF)
            query = qkv[pair, rows]
            outs = []
            for head in range(2):
                scores = dot(qkv[4 + pair], only(head, query), NT) * SCALE + bias[:, rows]
                scores = jnp.exp(scores - jnp.max(scores, axis=0, keepdims=True))
                weights = scores * (1.0 / jnp.sum(scores, axis=0, keepdims=True))
                weights = weights.astype(BF16)
                probs[2 * pair + head, :, rows] = weights
                outs.append(dot(weights, qkv[8 + pair], TN))
            ctx[pair, rows] = jnp.where(low_lanes, outs[0], outs[1]).astype(BF16)

    loop(2, attend)
    for route in range(ROUTES):
        late.wait_recv(route, 4)
        late.start(route, 5)
    loop(2, lambda pair: attend(pair + 2))
    for route in range(ROUTES):
        late.wait_recv(route, 5)

    terms_sent = []

    def row_terms(n, tiles, left):
        def block(rows, store):
            def one(k):
                lanes = pl.ds(pl.multiple_of(k * COLS, COLS), COLS)
                total = None
                for t, at in enumerate(tiles):
                    term = dot(left(t, rows), w[at, k].reshape(COLS, COLS), NT)
                    total = term if total is None else total + term
                store(lanes, total)

            loop(4, one)

        if n:
            terms_sent[-1].wait_send()

        def leaves(lanes, total):
            leave[:, lanes] = total.astype(BF16)

        def stays_here(lanes, total):
            part[:, lanes] = total

        block(other_rows, leaves)
        copy = to_twin(1 + n, leave, come)
        copy.start()
        block(own_rows, stays_here)
        copy.wait_recv()
        terms_sent.append(copy)

    def side_by_side(ref, first, rows=slice(None)):
        return jnp.concatenate([ref[first, rows], ref[first + 1, rows]], axis=1)

    sent = [rows_copy]
    row_terms(0, range(OUT_TILE, UP_TILE), lambda t, rows: side_by_side(ctx, 2 * t, rows))
    chunk = 64

    def by_chunks(body):
        def one(i):
            at = pl.multiple_of(i * chunk, chunk)
            body(pl.ds(at, chunk), pl.ds(pl.multiple_of(core * HALF + at, chunk), chunk))

        loop(HALF // chunk, one)

    def mean(values):
        return jnp.mean(values, axis=-1, keepdims=True)

    def normalized(hidden):
        centered = hidden - mean(hidden)
        scale = lax.rsqrt(mean(centered * centered) + EPSILON)
        return centered * scale, scale

    for n in range(6):
        sums[n] = jnp.zeros((1, WIDTH), F32)

    def add_sum(n, values):
        sums[n] += jnp.sum(values, axis=0, keepdims=True)

    b_out, b_down, gain_one, shift_one, gain_two, shift_two = range(6)

    def first_norm(here, there):
        hidden = x[there].astype(F32) + part[here] + come[here].astype(F32) + features[b_out]
        value, scale = normalized(hidden)
        hat[here] = value
        inv[here] = jnp.broadcast_to(scale, (chunk, 128))
        n1[there] = (value * features[gain_one] + features[shift_one]).astype(BF16)

    by_chunks(first_norm)

    shared = {}

    def share_rows(n, ref):
        copy = to_twin(n, ref.at[own_rows], ref.at[own_rows])
        copy.start()
        shared[n] = copy
        copy.wait_recv()

    share_rows(5, n1)

    def up(t):
        for half in range(2):
            rows = slice(half * HALF, half * HALF + HALF)
            pre = dot(n1[rows], weight(UP_TILE + t)) + biases[6 + t]
            below = 0.5 * (1.0 + lax.erf(pre * (0.5**0.5)))
            act[t, rows] = (pre * below).astype(BF16)
            bell = jnp.exp(pre * pre * -0.5) * 0.3989422804014327
            slope[t, rows] = (below + pre * bell).astype(BF16)

    loop(8, up)
    row_terms(1, range(DOWN_TILE, TILES), lambda t, rows: act[t, rows])
    swap_wait(*cot_move)

    def norm_back(values, incoming, gain, scale, gain_at, shift_at):
        add_sum(shift_at, incoming)
        add_sum(gain_at, incoming * values)
        scaled = incoming * gain
        return scale * (scaled - mean(scaled) - values * mean(scaled * values))

    def second_norm(here, there):
        first = hat[here] * features[gain_one] + features[shift_one]
        value, scale = normalized(first + part[here] + come[here].astype(F32) + features[b_down])
        live = jnp.where(segcol[there, 0:1] >= 0, 1.0, 0.0)
        out_rows[here] = ((value * features[gain_two] + features[shift_two]) * live).astype(BF16)
        back = norm_back(
            value, cot[here] * live, features[gain_two], scale, gain_two, shift_two
        )
        add_sum(b_down, back)
        d_two[here] = back
        gd[there] = back.astype(BF16)

    by_chunks(second_norm)
    out_move = (TILES + 3, out_rows, layer_out, layer_out)
    swap_start(*out_move)
    share_rows(6, gd)

    def turn(ref):
        for k in range(4):
            rows = slice(k * COLS, k * COLS + COLS)
            tr[rows, :] = ref[:, rows].T

    def store_grad(tile, right):
        for k in range(4):
            made = dot(tr[k * COLS : k * COLS + COLS, :], right)
            g[tile, k] = made.astype(BF16).reshape(4, 4, 16, COLS)

    scatter_late = Scatter(g, landings[:36], ssend, srecv, late_tiles)
    scatter_early = Scatter(g, landings[36:], ssend, srecv, early_tiles, COPIES)

    turn(gd)
    loop(8, lambda t: store_grad(DOWN_TILE + t, act[t]))
    for route in (5, 4):
        scatter_late.start(route, 0)

    def up_back(t):
        made = (dot(gd[...], weight(DOWN_TILE + t)) * slope[t].astype(F32)).astype(BF16)
        slope[t] = made
        bias_sums[6 + t] = jnp.sum(made.astype(F32), axis=0, keepdims=True)

    loop(8, up_back)
    turn(n1)
    loop(8, lambda t: store_grad(UP_TILE + t, slope[t]))
    for route in (3, 2, 1):
        scatter_late.start(route, 0)
    row_terms(2, range(UP_TILE, DOWN_TILE), lambda t, rows: slope[t, rows])

    def first_norm_back(here, there):
        incoming = d_two[here] + part[here] + come[here].astype(F32)
        back = norm_back(
            hat[here], incoming, features[gain_one], inv[here, 0:1], gain_one, shift_one
        )
        add_sum(b_out, back)
        d_two[here] = back
        n1[there] = back.astype(BF16)

    shared.pop(5).wait_send()
    d1 = n1
    by_chunks(first_norm_back)
    share_rows(7, d1)
    turn(d1)
    loop(2, lambda u: store_grad(OUT_TILE + u, side_by_side(ctx, 2 * u)))
    scatter_late.start(0, 0)

    def context_back(u):
        made = dot(d1[...], weight(OUT_TILE + u)).astype(BF16)
        gctx[2 * u] = made[:, :128]
        gctx[2 * u + 1] = made[:, 128:]

    loop(2, context_back)

    def attend_back(pair):
        for half in range(2):
            rows = slice(half * HALF, half * HALF + HALF)
            for head in range(2):
                weights = probs[2 * pair + head, :, rows].astype(F32)
                grad = dot(qkv[8 + pair], only(head, gctx[pair, rows]), NT)
                total = jnp.sum(grad * weights, axis=0, keepdims=True)
                ds[head, :, rows] = (weights * (grad - total)).astype(BF16)
        query = [dot(ds[head], qkv[4 + pair], TN) for head in range(2)]
        key = [dot(ds[head], qkv[pair]) for head in range(2)]
        value = [dot(probs[2 * pair + head], gctx[pair]) for head in range(2)]
        for at, (a, b), scale in ((0, query, SCALE), (4, key, SCALE), (8, value, 1.0)):
            made = (jnp.where(low_lanes, a, b) * scale).astype(BF16)
            qkv[at + pair] = made
            bias_sums[14 + at + pair, :, :PAIR] = jnp.sum(made.astype(F32), axis=0, keepdims=True)

    loop(4, attend_back)
    for route in range(ROUTES):
        scatter_late.take(route, 0)
        scatter_late.start(route, 1)
    turn(x)
    loop(6, lambda t: store_grad(t, side_by_side(qkv, 2 * t)))
    for route in range(ROUTES):
        scatter_early.start(route, 0)

    zero = jnp.zeros((1, 128), F32)
    kept_back[0] = jnp.zeros((VEC_ROWS, 128), F32)
    for k in range(4):
        kept_back[0, pl.ds(core * 4 + k, 1), :] = bias_sums[14 + k, :, :PAIR]
        kept_back[0, pl.ds(8 + core * 4 + k, 1), :] = bias_sums[22 + k, :, :PAIR]
    for k in range(8):
        for half in range(2):
            lanes = slice(half * 128, half * 128 + 128)
            kept_back[0, pl.ds(16 + core * 16 + k * 2 + half, 1), :] = bias_sums[6 + k, :, lanes]
    for n in range(6):
        for k in range(8):
            at = 48 + n * 8 + k
            kept_back[0, at : at + 1, :] = sums[n, :, k * 128 : k * 128 + 128]
    vectors_back = VectorSum(kept_back, came_back, vsend, vrecv, 7)
    vectors_back.start(0)
    row_terms(3, range(6), lambda t, rows: side_by_side(qkv, 2 * t, rows))

    def last_rows(here, there):
        cot[here] = d_two[here] + part[here] + come[here].astype(F32)

    by_chunks(last_rows)
    grad_move = (TILES + 4, cot, input_grad, input_grad)
    swap_start(*grad_move)

    for stage in range(1, 6):
        for route in range(ROUTES):
            scatter_late.take(route, stage)
            if stage < 5:
                scatter_late.start(route, stage + 1)
        for route in range(ROUTES):
            scatter_early.take(route, stage - 1)
            scatter_early.start(route, stage)
        vectors_back.take(stage - 1)
        vectors_back.start(stage)
    for route in range(ROUTES):
        scatter_early.take(route, 5)
    vectors_back.take(5)
    vectors_back.start(6)
    tile = 0
    grad_moves = []
    own_grads = (own_grads_q, own_grads_k, own_grads_v, own_grads_o, own_grads_u, own_grads_d)
    outs = (g_q, g_k, g_v, g_o, g_u, g_d)
    for n, (ref, out, count) in enumerate(zip(own_grads, outs, WEIGHT_TILES)):
        for k in range(count):
            ref[:, k * COLS : k * COLS + COLS] = g[tile, y, x_at, z].astype(F32)
            tile += 1
        grad_moves.append((TILES + 5 + n, ref, out, out))
        swap_start(*grad_moves[-1])
    vectors_back.take(6)
    vec_out[...] = kept_back[7]

    for move in [out_move, grad_move] + grad_moves:
        swap_wait(*move)
    for copy in sent + terms_sent[-1:] + list(shared.values()):
        copy.wait_send()
    for stage in range(6):
        for route in range(ROUTES):
            early.wait_send(route, stage)
            late.wait_send(route, stage)
            scatter_early.wait_send(route, stage)
            scatter_late.wait_send(route, stage)
    for stage in range(7):
        vectors.wait_send(stage)
        vectors_back.wait_send(stage)


def layer_call(*arrays):
    full = (TILES, 4, 4, 4, 16, COLS)
    vmem = functools.partial(pl.BlockSpec, memory_space=pltpu.VMEM)
    anywhere = functools.partial(pl.BlockSpec, memory_space=pl.ANY)
    rows = (GROUP, WIDTH)
    half = (HALF, WIDTH)
    shares = [(16, count * COLS) for count in WEIGHT_TILES]
    scratch = [
        (full, BF16), (full, BF16),
        (rows, BF16), (rows, BF16), (rows, BF16), ((WIDTH, GROUP), BF16),
        ((12, GROUP, PAIR), BF16), ((8, GROUP, GROUP), BF16), ((GROUP, GROUP), F32),
        ((4, GROUP, PAIR), BF16), ((4, GROUP, PAIR), BF16), ((2, GROUP, GROUP), BF16),
        (half, F32), (half, BF16), (half, BF16),
        (half, F32), ((HALF, 128), F32), (half, F32), (half, F32),
        ((8, GROUP, COLS), BF16), ((8, GROUP, COLS), BF16),
        ((8, GROUP), F32), ((GROUP, 128), F32),
        ((6, 1, WIDTH), F32), ((14, 1, COLS), F32), ((26, 1, COLS), F32), ((6, 1, WIDTH), F32),
        (half, BF16),
    ] + [(share, F32) for share in shares] + [
        ((8, VEC_ROWS, 128), F32), ((7, VEC_ROWS, 128), F32),
        ((8, VEC_ROWS, 128), F32), ((7, VEC_ROWS, 128), F32),
    ]
    sems = [2 * COPIES] * 4 + [14] * 2 + [TILES + 11] * 2 + [8] * 2
    return pl.pallas_call(
        layer_kernel,
        out_shape=(
            jax.ShapeDtypeStruct(half, BF16),
            jax.ShapeDtypeStruct(half, F32),
            *(jax.ShapeDtypeStruct(share, F32) for share in shares),
            jax.ShapeDtypeStruct((VEC_ROWS, 128), F32),
        ),
        in_specs=[vmem()] * 8 + [anywhere()] * 2,
        out_specs=(anywhere(),) * 2 + (vmem(),) * 7,
        scratch_shapes=[pltpu.VMEM(*s) for s in scratch]
        + [pltpu.SemaphoreType.DMA((n,)) for n in sems]
        + [pltpu.VMEM(s, BF16) for s in landing_shapes(late_tiles) + landing_shapes(early_tiles)],
        compiler_params=pltpu.CompilerParams(
            collective_id=0, has_side_effects=True, vmem_limit_bytes=64 * 2**20
        ),
    )(*arrays)


def packed_vectors(b_query, b_value, b_up, features):
    dp, low = lax.axis_index("dp"), lax.axis_index("tensor")
    own = jnp.arange(128)[:, None] == low * 64 + dp
    parts = [jnp.where(own, v.astype(F32)[None], 0.0).reshape(-1) for v in (b_query, b_value, b_up)]
    own = (jnp.arange(64)[:, None] == dp) & (low == 0)
    parts += [jnp.where(own, v.astype(F32)[None], 0.0).reshape(-1) for v in features]
    return jnp.concatenate(parts).reshape(VEC_ROWS, 128)


def unpacked_vectors(flat):
    dp, low = lax.axis_index("dp"), lax.axis_index("tensor")
    out, at = [], 0
    for length in (8, 8, 32):
        out.append(lax.dynamic_slice(flat, (at + (low * 64 + dp) * length,), (length,)))
        at += length * 128
    for _ in range(6):
        out.append(lax.dynamic_slice(flat, (at + dp * 16,), (16,)))
        at += 1024
    return out


def on_device(
    tokens, segment, w_query, w_key, w_value, w_out, w_up, w_down, b_query, b_value, b_up,
    b_out, b_down, gain_one, shift_one, gain_two, shift_two, out_grad,
):
    vec = packed_vectors(
        b_query, b_value, b_up, (b_out, b_down, gain_one, shift_one, gain_two, shift_two)
    )
    seg = jnp.broadcast_to(segment.astype(F32)[None], (8, GROUP))
    *outs, totals = layer_call(
        w_query, w_key, w_value, w_out, w_up, w_down, vec, seg, tokens, out_grad
    )
    return (*outs, *unpacked_vectors(totals.reshape(-1)))


def solution(mesh):
    placed = (
        P(("dp", "tensor"), None),
        P("dp"),
        P("dp", "tensor"),
        P("dp", "tensor"),
        P("dp", "tensor"),
        P("dp", "tensor"),
        P("dp", "tensor"),
        P("dp", "tensor"),
        P(("tensor", "dp")),
        P(("tensor", "dp")),
        P(("tensor", "dp")),
        P("dp"),
        P("dp"),
        P("dp"),
        P("dp"),
        P("dp"),
        P("dp"),
        P(("dp", "tensor"), None),
    )
    return jax.shard_map(
        on_device,
        mesh=mesh,
        in_specs=placed,
        out_specs=(
            P(("dp", "tensor"), None),
            P(("dp", "tensor"), None),
            P("dp", "tensor"),
            P("dp", "tensor"),
            P("dp", "tensor"),
            P("dp", "tensor"),
            P("dp", "tensor"),
            P("dp", "tensor"),
            P(("tensor", "dp")),
            P(("tensor", "dp")),
            P(("tensor", "dp")),
            P("dp"),
            P("dp"),
            P("dp"),
            P("dp"),
            P("dp"),
            P("dp"),
        ),
        check_vma=False,
    )
```

profile of v0, /device:TPU:1, one launch (start us, length us, event | category | flops | bytes accessed | tf_op | source)
XLA Modules:
  0.0 224.8 jit_solution(5252814939572677881)
XLA Ops:
  0.7 0.6 copy-done.8
  1.3 0.7 copy-done.9
  2.0 0.7 copy-done.10
  2.7 0.7 copy-done.11
  3.3 0.7 copy-done.12
  4.0 0.7 copy-done.13
  4.6 0.7 copy-done.14
  5.3 0.6 copy-done.15
  5.9 0.7 copy-done.7
  6.6 0.6 broadcast_in_dim.146.seg
  8.9 0.6 constant_dynamic-update-slice_fusion.6
  10.0 0.6 constant_dynamic-update-slice_fusion.5
  13.6 200.1 %shard_map.305 = (bf16[256,1024]{1,0:T(8,128)(2,1)}, f32[256,1024]{1,0:T(8,128)}, f32[16,512]{1,0:T(8,128)}, f32[16,512]{1,0:T(8,128)}, f32[16,512]{1,0:T(8,128)...) custom-call(bf16[16,512]{1,0:T(8,128)(2,1)} %w_q.1, bf16[16,512]{1,0:T(8,128)(2,1)} %w_k.1, ...), custom_call_target="tpu_custom_call" | custom-call | tf_op jit(solution)/shard_map/pallas_call | solution.py:706
  213.7 1.3 dynamic_slice.29
  215.1 1.3 fusion
  216.4 1.3 fusion.1
  217.7 1.9 copy.51
  219.5 1.0 copy.52
  220.5 0.6 copy.53
  221.1 0.6 copy.54
  221.8 0.6 copy.55
  222.5 0.6 copy.56
  223.2 0.7 copy.57
  224.1 0.7 copy.58
  (56 shorter events, 5.7 us)
Async XLA Ops:
  0.7 0.7 copy-start.8
  1.3 0.7 copy-start.9
  2.0 0.7 copy-start.10
  2.7 0.7 copy-start.11
  3.3 0.7 copy-start.12
  4.0 0.7 copy-start.13
  4.6 0.7 copy-start.14
  5.3 0.7 copy-start.15
  5.3 0.7 copy-start.16
  5.9 0.7 copy-start.7
  213.7 5.8 %copy-start = (f32[256,1024]{1,0:T(8,128)S(1)}, f32[256,1024]{1,0:T(8,128)}, u32[]{:S(2)}) copy-start(f32[256,1024]{1,0:T(8,128)} %get-tuple-element.69) | copy-start | bytes 3145732
  219.5 1.0 copy-start.6
  219.5 1.6 copy-start.5
  219.5 2.2 copy-start.4
  220.5 2.6 %copy-start.2 = (f32[16,2048]{1,0:T(8,128)S(1)}, f32[16,2048]{1,0:T(8,128)}, u32[]{:S(2)}) copy-start(f32[16,2048]{1,0:T(8,128)} %get-tuple-element.74) | copy-start | bytes 393220
  221.8 0.8 copy-start.3
  223.1 1.0 copy-start.1
where the time goes:
time: 225 us
  Pallas kernels  200 us (89%)
  local copies, waits for them, and re-layouts  23.6 us (10%)
    pallas_call x1, Pallas kernels, layer_call(): pl.pallas_call(layer_kernel, out_shape=(jax.ShapeDtypeStruct(half, BF16),...  200 us
    unnamed x50, local copies, waits for them, and re-layouts  17.7 us

commit v1 on v0

v1 whole, which is shorter than its diff:
```python
import jax
import jax.numpy as jnp
from jax import lax
from jax.experimental import pallas as pl
from jax.experimental.pallas import tpu as pltpu
from jax.sharding import PartitionSpec as P

MESH = pl.DeviceIdType.MESH
F32 = jnp.float32
BF16 = jnp.bfloat16

TILES = 24
COLS = 256
PHASES, ROUTES, STEPS = 4, 3, 6
VEC_ROWS = 96
ORDERS = ((2, 0, 1), (1, 2, 0), (0, 1, 2))


def position():
    dp, low = lax.axis_index("dp"), lax.axis_index("tensor")
    return (dp // 16, lax.rem(dp // 4, 4), lax.rem(dp // 2, 2) * 2 + low), lax.rem(dp, 2)


def device(chip, core):
    y, x, z = chip
    return (y * 16 + x * 4 + (z // 2) * 2 + core, lax.rem(z, 2))


def moved(chip, axis, by):
    return tuple(lax.rem(c + by, 4) if k == axis else c for k, c in enumerate(chip))


def opposite_z(chip):
    y, x, z = chip
    return (y, x, z + 1 - 2 * lax.rem(z, 2))


def blocks(chip, full):
    return tuple(pl.ds(0, 4) if axis in full else pl.ds(c, 1) for axis, c in enumerate(chip))


def block_shape(full):
    return tuple(4 if axis in full else 1 for axis in range(3))


def first_tile(phase, route):
    return phase * 6 + route * 2


class Ring:
    def __init__(self, sems):
        self.send, self.recv = sems
        self.chip, self.core = position()

    def copy(self, phase, route, step, way, axis, src, dst):
        sem = ((phase * ROUTES + route) * STEPS + step) * 2 + way
        target = device(moved(self.chip, axis, 1 if way == 0 else 3), self.core)
        return pltpu.make_async_remote_copy(
            src_ref=src, dst_ref=dst, send_sem=self.send.at[sem], recv_sem=self.recv.at[sem],
            device_id=target, device_id_type=MESH,
        )

    def start(self, phase, route, step):
        for c in self.copies(phase, route, step):
            c.start()

    def wait_recv(self, phase, route, step):
        for c in self.copies(phase, route, step):
            c.wait_recv()

    def wait_send(self, phase, route, step):
        for c in self.copies(phase, route, step):
            c.wait_send()


class Gather(Ring):
    def __init__(self, w, sems):
        super().__init__(sems)
        self.w = w

    def copies(self, phase, route, step):
        order = ORDERS[route]
        axis, full = order[step // 2], order[: step // 2]
        tile = first_tile(phase, route)
        out = []
        for way in range(2):
            if step % 2 == 0:
                part = self.w.at[(pl.ds(tile, 2),) + blocks(self.chip, full)]
            else:
                behind = moved(self.chip, axis, 3 if way == 0 else 1)
                part = self.w.at[(pl.ds(tile + way, 1),) + blocks(behind, full)]
            out.append(self.copy(phase, route, step, way, axis, part, part))
        return out

    def step(self, phase, step):
        for route in range(ROUTES):
            if step:
                self.wait_recv(phase, route, step - 1)
            if step < STEPS:
                self.start(phase, route, step)


def landing_shapes():
    shapes = []
    for _ in range(PHASES):
        for order in ORDERS:
            for k in range(3):
                shapes.append((6,) + block_shape(order[: 2 - k]) + (16, COLS))
    return shapes


class Scatter(Ring):
    def __init__(self, g, landings, sems):
        super().__init__(sems)
        self.g, self.landings = g, landings

    def at(self, route, step):
        order = ORDERS[route]
        return order[2 - step // 2], order[: 2 - step // 2]

    def landing(self, phase, route, step):
        return self.landings[(phase * ROUTES + route) * 3 + step // 2]

    def copies(self, phase, route, step):
        axis, full = self.at(route, step)
        tile = first_tile(phase, route)
        landed = self.landing(phase, route, step)
        out = []
        for way in range(2):
            if step % 2 == 0:
                src = self.g.at[(pl.ds(tile + way, 1),) + blocks(moved(self.chip, axis, 2), full)]
                dst = landed.at[pl.ds(way, 1)]
            else:
                ahead = moved(self.chip, axis, 1 if way == 0 else 3)
                src = self.g.at[(pl.ds(tile, 2),) + blocks(ahead, full)]
                dst = landed.at[pl.ds(2 + 2 * way, 2)]
            out.append(self.copy(phase, route, step, way, axis, src, dst))
        return out

    def take(self, phase, route, step):
        self.wait_recv(phase, route, step)
        axis, full = self.at(route, step)
        tile = first_tile(phase, route)
        landed = self.landing(phase, route, step)
        ny, nx, nz = block_shape(full)

        def start_of(chip):
            return tuple(0 if k in full else c for k, c in enumerate(chip))

        def add(t, base, parts):
            y0, x0, z0 = base

            def one(i, carry):
                at = (tile + t, y0 + i, pl.ds(x0, nx), pl.ds(z0, nz))
                total = self.g[at].astype(F32)
                for part in parts:
                    total += landed[part, i].astype(F32)
                self.g[at] = total.astype(BF16)
                return carry

            lax.fori_loop(0, ny, one, 0)

        for t in range(2):
            if step % 2 == 0:
                add(t, start_of(moved(self.chip, axis, 1 if t == 0 else 3)), (t,))
            else:
                add(t, start_of(self.chip), (2 + t, 4 + t))

    def step(self, phase, step):
        for route in range(ROUTES):
            if step:
                self.take(phase, route, step - 1)
            if step < STEPS:
                self.start(phase, route, step)


def greet(others):
    barrier = pltpu.get_barrier_semaphore()
    for other in others:
        pl.semaphore_signal(barrier, inc=1, device_id=other, device_id_type=MESH)
    pl.semaphore_wait(barrier, len(others))


def sibling():
    chip, core = position()
    return device(chip, 1 - core)


def vector_partner(stage):
    chip, core = position()
    if stage == 0:
        return device(chip, 1 - core)
    axis = (stage - 1) // 2
    c = chip[axis]
    new = c + 1 - 2 * lax.rem(c, 2) if stage % 2 else 3 - c
    return device(tuple(new if k == axis else v for k, v in enumerate(chip)), core)


class VectorSum:
    def __init__(self, kept, came, sems, base):
        self.kept, self.came, (self.send, self.recv), self.base = kept, came, sems, base

    def copy(self, stage):
        return pltpu.make_async_remote_copy(
            src_ref=self.kept.at[stage],
            dst_ref=self.came.at[stage],
            send_sem=self.send.at[self.base + stage],
            recv_sem=self.recv.at[self.base + stage],
            device_id=vector_partner(stage),
            device_id_type=MESH,
        )

    def step(self, stage):
        if stage:
            self.copy(stage - 1).wait_recv()
            self.kept[stage] = self.kept[stage - 1] + self.came[stage - 1]
        if stage < 7:
            self.copy(stage).start()

    def wait_send(self, stage):
        self.copy(stage).wait_send()


GROUP = 512
HALF = 256
WIDTH = 1024
HEAD_DIM = 64
PAIR = 2 * HEAD_DIM
SCALE = HEAD_DIM**-0.5
EPSILON = 1e-12
NN = (((1,), (0,)), ((), ()))
NT = (((1,), (1,)), ((), ()))
TN = (((0,), (0,)), ((), ()))
Q_TILE, OUT_TILE, UP_TILE, DOWN_TILE = 0, 6, 8, 16
WEIGHT_TILES = (2, 2, 2, 2, 8, 8)


def dot(a, b, dims=NN):
    return lax.dot_general(a, b, dims, preferred_element_type=F32)


def loop(count, body):
    def step(i, carry):
        body(i)
        return carry

    lax.fori_loop(0, count, step, 0)


VECTORS = (8, 8, 32, 16, 16, 16, 16, 16, 16)
VECTOR_ROWS = (0, 8, 16, 48, 56, 64, 72, 80, 88)


def layer_kernel(
    w_q, w_k, w_v, w_o, w_u, w_d,
    v_0, v_1, v_2, v_3, v_4, v_5, v_6, v_7, v_8, segment, tokens, out_grad,
    layer_out, input_grad, shares, vec_out,
    w, g, x, n1, gd, tr, qkv, probs, bias, ctx, gctx, ds, part, leave, come,
    hat, inv, d_two, cot, act, slope, seg_here, seg_own, segments, segcol, features, biases, bias_sums, sums, out_rows,
    r_0, r_1, r_2, r_3, r_4, r_5, r_6, r_7, r_8, placed,
    kept, came, kept_front, came_front, kept_tail, came_tail,
    gsend, grecv, ssend, srecv, vsend, vrecv, swap_send, swap_recv, sib_send, sib_recv, load_sem,
    *landings,
):
    chip, core = position()
    y, x_at, z = chip
    low = lax.rem(z, 2)
    opposite_chip = opposite_z(chip)
    diagonal = device(opposite_chip, 1 - core)
    twin = sibling()
    stays = core == low
    own_rows = pl.ds(pl.multiple_of(core * HALF, HALF), HALF)
    other_rows = pl.ds(pl.multiple_of((1 - core) * HALF, HALF), HALF)

    raw = (r_0, r_1, r_2, r_3, r_4, r_5, r_6, r_7, r_8)
    loads = [
        pltpu.make_async_copy(src, dst, load_sem.at[n])
        for n, (src, dst) in enumerate(zip((v_0, v_1, v_2, v_3, v_4, v_5, v_6, v_7, v_8), raw))
    ]
    loads.append(pltpu.make_async_copy(segment, seg_here.at[0], load_sem.at[9]))
    loads.append(pltpu.make_async_copy(out_grad, d_two, load_sem.at[10]))
    for load in loads:
        load.start()

    def swap_copies(n, src, dst_here, dst_there):
        away = pltpu.make_async_remote_copy(
            src_ref=src, dst_ref=dst_there, send_sem=swap_send.at[n], recv_sem=swap_recv.at[n],
            device_id=diagonal, device_id_type=MESH,
        )
        return away, pltpu.make_async_copy(src, dst_here, swap_recv.at[n])

    def swap_start(n, src, dst_here, dst_there):
        away, here = swap_copies(n, src, dst_here, dst_there)
        pl.when(stays)(here.start)
        pl.when(jnp.logical_not(stays))(away.start)

    def swap_wait(n, src, dst_here, dst_there):
        away, here = swap_copies(n, src, dst_here, dst_there)
        pl.when(stays)(here.wait)
        pl.when(jnp.logical_not(stays))(away.wait)

    def to_twin(n, src, dst):
        return pltpu.make_async_remote_copy(
            src_ref=src, dst_ref=dst, send_sem=sib_send.at[n], recv_sem=sib_recv.at[n],
            device_id=twin, device_id_type=MESH,
        )

    greet([device(moved(chip, axis, by), core) for axis in range(3) for by in (1, 3)] + [twin, diagonal])

    weight_moves = []
    tile = 0
    for ref, count in zip((w_q, w_k, w_v, w_o, w_u, w_d), WEIGHT_TILES):
        for k in range(count):
            weight_moves.append(
                (
                    tile,
                    ref.at[:, pl.ds(k * COLS, COLS)],
                    w.at[tile, y, x_at, z],
                    w.at[(tile,) + opposite_chip],
                )
            )
            tile += 1
    for move in weight_moves[:6]:
        swap_start(*move)
    row_move = (TILES, tokens, x.at[own_rows], x.at[other_rows])
    swap_start(*row_move)
    for move in weight_moves[6:]:
        swap_start(*move)

    gather = Gather(w, (gsend, grecv))
    vectors = VectorSum(kept, came, (vsend, vrecv), 0)

    def arrived(phase):
        for move in weight_moves[6 * phase : 6 * phase + 6]:
            swap_wait(*move)

    arrived(0)
    gather.step(0, 0)

    for load in loads:
        load.wait()
    dp, tensor = lax.axis_index("dp"), lax.axis_index("tensor")
    placed[...] = jnp.zeros((VEC_ROWS, 128), F32)
    for n, (ref, length, row) in enumerate(zip(raw, VECTORS, VECTOR_ROWS)):
        at = (tensor * 64 + dp if n < 3 else dp) * length
        value = ref[...].astype(F32).reshape(1, length)
        value = jnp.concatenate([value, jnp.zeros((1, 128 - length), F32)], axis=1)
        value = pltpu.roll(jnp.broadcast_to(value, (8, 128)), lax.rem(at, 128), 1)
        if n >= 3:
            value = jnp.where(tensor == 0, value, 0.0)
        placed[pl.ds(row + at // 128, 1), :] = value[0:1]
    kept[0] = placed[...].astype(BF16)
    vectors.step(0)
    seg_own[...] = jnp.broadcast_to(seg_here[...].astype(F32), (8, GROUP))
    seg_move = (TILES + 1, seg_own, segments, segments)
    swap_start(*seg_move)

    gather.step(0, 1)
    vectors.step(1)
    arrived(1)
    gather.step(1, 0)
    swap_wait(*row_move)
    rows_copy = to_twin(0, x.at[own_rows], x.at[own_rows])
    rows_copy.start()
    gather.step(0, 2)
    vectors.step(2)
    gather.step(1, 1)
    arrived(2)
    gather.step(2, 0)
    gather.step(0, 3)
    vectors.step(3)
    gather.step(1, 2)
    gather.step(2, 1)
    arrived(3)
    gather.step(0, 4)
    vectors.step(4)
    gather.step(1, 3)
    gather.step(2, 2)
    gather.step(3, 0)
    vectors.step(5)

    swap_wait(*seg_move)
    across_lanes = jnp.broadcast_to(segments[0:1, :], (128, GROUP))
    segcol[...] = across_lanes.T
    for k in range(4):
        cols = slice(k * 128, k * 128 + 128)
        bias[:, cols] = jnp.where(segcol[...] == segments[0:1, cols], 0.0, -1000000000.0)
    vectors.step(6)
    gather.step(0, 5)
    gather.step(1, 4)
    gather.step(2, 3)
    gather.step(3, 1)
    vectors.step(7)
    placed[...] = kept[7].astype(F32)
    for n in range(6):
        for k in range(8):
            features[n, :, k * 128 : k * 128 + 128] = placed[48 + n * 8 + k : 49 + n * 8 + k, :]
    for k in range(2):
        for half in range(2):
            lanes = slice(half * 128, half * 128 + 128)
            biases[k, :, lanes] = placed[pl.ds(core * 4 + k * 2 + half, 1), :]
            biases[4 + k, :, lanes] = placed[pl.ds(8 + core * 4 + k * 2 + half, 1), :]
        biases[2 + k] = jnp.zeros((1, COLS), F32)
    for k in range(8):
        for half in range(2):
            lanes = slice(half * 128, half * 128 + 128)
            biases[6 + k, :, lanes] = placed[pl.ds(16 + core * 16 + k * 2 + half, 1), :]
    rows_copy.wait_recv()
    out_rows[...] = d_two[...].astype(BF16)
    gather.step(0, 6)

    def weight(tile):
        return w[tile].reshape(WIDTH, COLS)

    def project(t):
        made = (dot(x[...], weight(t)) + biases[t]).astype(BF16)
        qkv[2 * t] = made[:, :128]
        qkv[2 * t + 1] = made[:, 128:]

    loop(6, project)
    gather.step(2, 4)
    gather.step(3, 2)
    low_lanes = lax.broadcasted_iota(jnp.int32, (1, PAIR), 1) < HEAD_DIM

    def only(head, values):
        keep = low_lanes if head == 0 else jnp.logical_not(low_lanes)
        return jnp.where(keep, values, jnp.zeros_like(values))

    def attend(pair):
        for half in range(2):
            rows = slice(half * HALF, half * HALF + HALF)
            query = qkv[pair, rows]
            outs = []
            for head in range(2):
                scores = dot(qkv[4 + pair], only(head, query), NT) * SCALE + bias[:, rows]
                scores = jnp.exp(scores - jnp.max(scores, axis=0, keepdims=True))
                weights = scores * (1.0 / jnp.sum(scores, axis=0, keepdims=True))
                weights = weights.astype(BF16)
                probs[2 * pair + head, :, rows] = weights
                outs.append(dot(weights, qkv[8 + pair], TN))
            ctx[pair, rows] = jnp.where(low_lanes, outs[0], outs[1]).astype(BF16)

    attend(0)
    gather.step(1, 5)
    gather.step(2, 5)
    gather.step(3, 3)
    attend(1)
    gather.step(3, 4)
    attend(2)
    cot_move = (TILES + 2, out_rows, cot, cot)
    swap_start(*cot_move)
    attend(3)
    gather.step(1, 6)
    gather.step(3, 5)

    terms_sent = []

    def row_terms(n, tiles, left):
        def block(rows, store):
            def one(k):
                lanes = pl.ds(pl.multiple_of(k * COLS, COLS), COLS)
                total = None
                for t, at in enumerate(tiles):
                    term = dot(left(t, rows), w[at, k].reshape(COLS, COLS), NT)
                    total = term if total is None else total + term
                store(lanes, total)

            loop(4, one)

        if n:
            terms_sent[-1].wait_send()

        def leaves(lanes, total):
            leave[:, lanes] = total.astype(BF16)

        def stays_here(lanes, total):
            part[:, lanes] = total

        block(other_rows, leaves)
        copy = to_twin(1 + n, leave, come)
        copy.start()
        block(own_rows, stays_here)
        copy.wait_recv()
        terms_sent.append(copy)

    def side_by_side(ref, first, rows=slice(None)):
        return jnp.concatenate([ref[first, rows], ref[first + 1, rows]], axis=1)

    sent = [rows_copy]
    row_terms(0, range(OUT_TILE, UP_TILE), lambda t, rows: side_by_side(ctx, 2 * t, rows))
    chunk = 64

    def by_chunks(body):
        def one(i):
            at = pl.multiple_of(i * chunk, chunk)
            body(pl.ds(at, chunk), pl.ds(pl.multiple_of(core * HALF + at, chunk), chunk))

        loop(HALF // chunk, one)

    def mean(values):
        return jnp.mean(values, axis=-1, keepdims=True)

    def normalized(hidden):
        centered = hidden - mean(hidden)
        scale = lax.rsqrt(mean(centered * centered) + EPSILON)
        return centered * scale, scale

    for n in range(6):
        sums[n] = jnp.zeros((1, WIDTH), F32)

    def add_sum(n, values):
        sums[n] += jnp.sum(values, axis=0, keepdims=True)

    b_out, b_down, gain_one, shift_one, gain_two, shift_two = range(6)

    def first_norm(here, there):
        hidden = x[there].astype(F32) + part[here] + come[here].astype(F32) + features[b_out]
        value, scale = normalized(hidden)
        hat[here] = value
        inv[here] = jnp.broadcast_to(scale, (chunk, 128))
        n1[there] = (value * features[gain_one] + features[shift_one]).astype(BF16)

    by_chunks(first_norm)

    shared = {}

    def share_rows(n, ref):
        copy = to_twin(n, ref.at[own_rows], ref.at[own_rows])
        copy.start()
        shared[n] = copy
        copy.wait_recv()

    share_rows(5, n1)

    def up(t):
        for half in range(2):
            rows = slice(half * HALF, half * HALF + HALF)
            pre = dot(n1[rows], weight(UP_TILE + t)) + biases[6 + t]
            below = 0.5 * (1.0 + lax.erf(pre * (0.5**0.5)))
            act[t, rows] = (pre * below).astype(BF16)
            bell = jnp.exp(pre * pre * -0.5) * 0.3989422804014327
            slope[t, rows] = (below + pre * bell).astype(BF16)

    loop(4, up)
    gather.step(2, 6)
    loop(4, lambda t: up(t + 4))
    gather.step(3, 6)
    row_terms(1, range(DOWN_TILE, TILES), lambda t, rows: act[t, rows])
    swap_wait(*cot_move)

    def norm_back(values, incoming, gain, scale, gain_at, shift_at):
        add_sum(shift_at, incoming)
        add_sum(gain_at, incoming * values)
        scaled = incoming * gain
        return scale * (scaled - mean(scaled) - values * mean(scaled * values))

    def second_norm(here, there):
        first = hat[here] * features[gain_one] + features[shift_one]
        value, scale = normalized(first + part[here] + come[here].astype(F32) + features[b_down])
        live = jnp.where(segcol[there, 0:1] >= 0, 1.0, 0.0)
        out_rows[here] = ((value * features[gain_two] + features[shift_two]) * live).astype(BF16)
        back = norm_back(
            value, cot[here].astype(F32) * live, features[gain_two], scale, gain_two, shift_two
        )
        add_sum(b_down, back)
        d_two[here] = back
        gd[there] = back.astype(BF16)

    by_chunks(second_norm)
    out_move = (TILES + 3, out_rows, layer_out, layer_out)
    swap_start(*out_move)
    share_rows(6, gd)

    def turn(ref):
        for k in range(4):
            rows = slice(k * COLS, k * COLS + COLS)
            tr[rows, :] = ref[:, rows].T

    def store_grad(tile, right):
        for k in range(4):
            made = dot(tr[k * COLS : k * COLS + COLS, :], right)
            g[tile, k] = made.astype(BF16).reshape(4, 4, 16, COLS)

    scatter = Scatter(g, landings, (ssend, srecv))
    share_moves = []

    def reduced(phase):
        scatter.step(phase, 6)
        tiles = pl.ds(6 * phase, 6)
        share_moves.append(
            (TILES + 5 + phase, g.at[tiles, y, x_at, z], shares.at[tiles], shares.at[tiles])
        )
        swap_start(*share_moves[-1])

    turn(gd)
    loop(8, lambda t: store_grad(DOWN_TILE + t, act[t]))
    scatter.step(3, 0)

    def up_back(t):
        made = (dot(gd[...], weight(DOWN_TILE + t)) * slope[t].astype(F32)).astype(BF16)
        slope[t] = made
        bias_sums[6 + t] = jnp.sum(made.astype(F32), axis=0, keepdims=True)

    loop(8, up_back)
    scatter.step(3, 1)
    turn(n1)
    loop(4, lambda t: store_grad(UP_TILE + 4 + t, slope[4 + t]))
    scatter.step(2, 0)
    loop(4, lambda t: store_grad(UP_TILE + t, slope[t]))
    scatter.step(3, 2)
    row_terms(2, range(UP_TILE, DOWN_TILE), lambda t, rows: slope[t, rows])

    def first_norm_back(here, there):
        incoming = d_two[here] + part[here] + come[here].astype(F32)
        back = norm_back(
            hat[here], incoming, features[gain_one], inv[here, 0:1], gain_one, shift_one
        )
        add_sum(b_out, back)
        d_two[here] = back
        n1[there] = back.astype(BF16)

    shared.pop(5).wait_send()
    d1 = n1
    scatter.step(2, 1)
    by_chunks(first_norm_back)
    share_rows(7, d1)
    turn(d1)
    loop(2, lambda u: store_grad(OUT_TILE + u, side_by_side(ctx, 2 * u)))
    scatter.step(1, 0)
    scatter.step(2, 2)
    scatter.step(3, 3)

    kept_front[0] = jnp.zeros((VEC_ROWS - 16, 128), F32)
    for k in range(8):
        for half in range(2):
            lanes = slice(half * 128, half * 128 + 128)
            kept_front[0, pl.ds(core * 16 + k * 2 + half, 1), :] = bias_sums[6 + k, :, lanes]
    for n in range(6):
        for k in range(8):
            at = 32 + n * 8 + k
            kept_front[0, at : at + 1, :] = sums[n, :, k * 128 : k * 128 + 128]
    front = VectorSum(kept_front, came_front, (vsend, vrecv), 7)
    front.step(0)

    def context_back(u):
        made = dot(d1[...], weight(OUT_TILE + u)).astype(BF16)
        gctx[2 * u] = made[:, :128]
        gctx[2 * u + 1] = made[:, 128:]

    loop(2, context_back)
    scatter.step(1, 1)
    scatter.step(3, 4)
    front.step(1)

    def attend_back(pair):
        for half in range(2):
            rows = slice(half * HALF, half * HALF + HALF)
            for head in range(2):
                weights = probs[2 * pair + head, :, rows].astype(F32)
                grad = dot(qkv[8 + pair], only(head, gctx[pair, rows]), NT)
                total = jnp.sum(grad * weights, axis=0, keepdims=True)
                ds[head, :, rows] = (weights * (grad - total)).astype(BF16)
        query = [dot(ds[head], qkv[4 + pair], TN) for head in range(2)]
        key = [dot(ds[head], qkv[pair]) for head in range(2)]
        value = [dot(probs[2 * pair + head], gctx[pair]) for head in range(2)]
        for at, (a, b), scale in ((0, query, SCALE), (4, key, SCALE), (8, value, 1.0)):
            made = (jnp.where(low_lanes, a, b) * scale).astype(BF16)
            qkv[at + pair] = made
            bias_sums[14 + at + pair, :, :PAIR] = jnp.sum(made.astype(F32), axis=0, keepdims=True)

    attend_back(0)
    scatter.step(2, 3)
    scatter.step(1, 2)
    scatter.step(3, 5)
    front.step(2)
    attend_back(1)
    scatter.step(2, 4)
    scatter.step(1, 3)
    reduced(3)
    front.step(3)
    attend_back(2)
    scatter.step(2, 5)
    scatter.step(1, 4)
    front.step(4)
    attend_back(3)
    kept_tail[0] = jnp.zeros((16, 128), F32)
    for k in range(4):
        kept_tail[0, pl.ds(core * 4 + k, 1), :] = bias_sums[14 + k, :, :PAIR]
        kept_tail[0, pl.ds(8 + core * 4 + k, 1), :] = bias_sums[22 + k, :, :PAIR]
    tail = VectorSum(kept_tail, came_tail, (vsend, vrecv), 14)
    tail.step(0)
    turn(x)
    loop(6, lambda t: store_grad(t, side_by_side(qkv, 2 * t)))
    scatter.step(0, 0)
    scatter.step(1, 5)
    reduced(2)
    tail.step(1)
    front.step(5)
    row_terms(3, range(6), lambda t, rows: side_by_side(qkv, 2 * t, rows))
    scatter.step(0, 1)
    tail.step(2)
    front.step(6)

    def last_rows(here, there):
        cot[here] = (d_two[here] + part[here] + come[here].astype(F32)).astype(BF16)

    by_chunks(last_rows)
    grad_move = (TILES + 4, cot, input_grad, input_grad)
    swap_start(*grad_move)
    scatter.step(0, 2)
    tail.step(3)
    front.step(7)
    reduced(1)
    scatter.step(0, 3)
    tail.step(4)
    scatter.step(0, 4)
    tail.step(5)
    scatter.step(0, 5)
    tail.step(6)
    reduced(0)
    tail.step(7)
    vec_out[0:16] = kept_tail[7]
    vec_out[16:] = kept_front[7]

    for move in [out_move, grad_move] + share_moves:
        swap_wait(*move)
    for copy in sent + terms_sent[-1:] + list(shared.values()):
        copy.wait_send()
    for phase in range(PHASES):
        for route in range(ROUTES):
            for step in range(STEPS):
                gather.wait_send(phase, route, step)
                scatter.wait_send(phase, route, step)
    for stage in range(7):
        vectors.wait_send(stage)
        front.wait_send(stage)
        tail.wait_send(stage)


def layer_call(*arrays):
    full = (TILES, 4, 4, 4, 16, COLS)
    rows = (GROUP, WIDTH)
    half = (HALF, WIDTH)
    front = VEC_ROWS - 16
    scratch = [
        (full, BF16), (full, BF16),
        (rows, BF16), (rows, BF16), (rows, BF16), ((WIDTH, GROUP), BF16),
        ((12, GROUP, PAIR), BF16), ((8, GROUP, GROUP), BF16), ((GROUP, GROUP), F32),
        ((4, GROUP, PAIR), BF16), ((4, GROUP, PAIR), BF16), ((2, GROUP, GROUP), BF16),
        (half, F32), (half, BF16), (half, BF16),
        (half, F32), ((HALF, 128), F32), (half, F32), (half, BF16),
        ((8, GROUP, COLS), BF16), ((8, GROUP, COLS), BF16),
        ((1, GROUP), jnp.int32), ((8, GROUP), F32), ((8, GROUP), F32), ((GROUP, 128), F32),
        ((6, 1, WIDTH), F32), ((14, 1, COLS), F32), ((26, 1, COLS), F32), ((6, 1, WIDTH), F32),
        (half, BF16),
    ] + [((length,), BF16) for length in VECTORS] + [
        ((VEC_ROWS, 128), F32),
        ((8, VEC_ROWS, 128), BF16), ((7, VEC_ROWS, 128), BF16),
        ((8, front, 128), F32), ((7, front, 128), F32),
        ((8, 16, 128), F32), ((7, 16, 128), F32),
    ]
    sems = [PHASES * ROUTES * STEPS * 2] * 4 + [21] * 2 + [TILES + 9] * 2 + [8] * 2 + [11]
    return pl.pallas_call(
        layer_kernel,
        out_shape=(
            jax.ShapeDtypeStruct(half, BF16),
            jax.ShapeDtypeStruct(half, BF16),
            jax.ShapeDtypeStruct((TILES, 16, COLS), BF16),
            jax.ShapeDtypeStruct((VEC_ROWS, 128), F32),
        ),
        in_specs=[pl.BlockSpec(memory_space=pl.ANY)] * len(arrays),
        out_specs=(pl.BlockSpec(memory_space=pl.ANY),) * 3 + (pl.BlockSpec(memory_space=pltpu.VMEM),),
        scratch_shapes=[pltpu.VMEM(*s) for s in scratch]
        + [pltpu.SemaphoreType.DMA((n,)) for n in sems]
        + [pltpu.VMEM(s, BF16) for s in landing_shapes()],
        compiler_params=pltpu.CompilerParams(
            collective_id=0, has_side_effects=True, vmem_limit_bytes=64 * 2**20
        ),
    )(*arrays)


def unpacked_vectors(flat):
    dp, low = lax.axis_index("dp"), lax.axis_index("tensor")
    out, at = [], 0
    for length in (8, 8, 32):
        out.append(lax.dynamic_slice(flat, (at + (low * 64 + dp) * length,), (length,)))
        at += length * 128
    for _ in range(6):
        out.append(lax.dynamic_slice(flat, (at + dp * 16,), (16,)))
        at += 1024
    return out


def on_device(
    tokens, segment, w_query, w_key, w_value, w_out, w_up, w_down, b_query, b_value, b_up,
    b_out, b_down, gain_one, shift_one, gain_two, shift_two, out_grad,
):
    layer_out, input_grad, shares, totals = layer_call(
        w_query, w_key, w_value, w_out, w_up, w_down, b_query, b_value, b_up,
        b_out, b_down, gain_one, shift_one, gain_two, shift_two, segment, tokens, out_grad,
    )
    shares = shares.astype(F32).transpose(1, 0, 2).reshape(16, TILES * COLS)
    ends = [sum(WEIGHT_TILES[:k]) * COLS for k in range(1, 6)]
    return (
        layer_out,
        input_grad.astype(F32),
        *jnp.split(shares, ends, axis=1),
        *unpacked_vectors(totals.reshape(-1)),
    )


def solution(mesh):
    placed = (
        P(("dp", "tensor"), None),
        P("dp"),
        P("dp", "tensor"),
        P("dp", "tensor"),
        P("dp", "tensor"),
        P("dp", "tensor"),
        P("dp", "tensor"),
        P("dp", "tensor"),
        P(("tensor", "dp")),
        P(("tensor", "dp")),
        P(("tensor", "dp")),
        P("dp"),
        P("dp"),
        P("dp"),
        P("dp"),
        P("dp"),
        P("dp"),
        P(("dp", "tensor"), None),
    )
    return jax.shard_map(
        on_device,
        mesh=mesh,
        in_specs=placed,
        out_specs=(
            P(("dp", "tensor"), None),
            P(("dp", "tensor"), None),
            P("dp", "tensor"),
            P("dp", "tensor"),
            P("dp", "tensor"),
            P("dp", "tensor"),
            P("dp", "tensor"),
            P("dp", "tensor"),
            P(("tensor", "dp")),
            P(("tensor", "dp")),
            P(("tensor", "dp")),
            P("dp"),
            P("dp"),
            P("dp"),
            P("dp"),
            P("dp"),
            P("dp"),
        ),
        check_vma=False,
    )
```

time: 225 us -> 194 us (0.86)
  local copies, waits for them, and re-layouts: 23.6 us -> 6.03 us
  Pallas kernels: 200 us -> 185 us
    unnamed x50 -> x5, local copies, waits for them, and re-layouts: 17.7 us -> 0.8 us
    pallas_call x1, Pallas kernels: 200 us -> 185 us  [layer_call(): pl.pallas_call(layer_kernel, out_shape=(jax.ShapeDtypeStruct(half, BF16),...]
where the time goes in v1:
time: 194 us
  Pallas kernels  185 us (95%)
  local copies, waits for them, and re-layouts  6.03 us (3%)
  other arithmetic  2.2 us (1%)
    pallas_call x1, Pallas kernels, layer_call(): pl.pallas_call(layer_kernel, out_shape=(jax.ShapeDtypeStruct(half, BF16),...  185 us

profile of v1, /device:TPU:1, one launch (start us, length us, event | category | flops | bytes accessed | tf_op | source)
XLA Modules:
  0.0 193.6 jit_solution(8904222189049016769)
XLA Ops:
  0.7 184.7 %shard_map.305 = (bf16[256,1024]{1,0:T(8,128)(2,1)}, bf16[256,1024]{1,0:T(8,128)(2,1)}, bf16[24,16,256]{2,1,0:T(8,128)(2,1)}, f32[96,128]{1,0:T(8,128)}) custom-call(bf16[16,512]{1,0:T(8,128)(2,1)} %w_q.1, bf16[16,512]{1,0:T(8,128)(2,1)} %w_k.1, bf16[16,512]{1,0:T(8,128)(2,1)} %w_v.1, bf16[16,512]{1,0:T(8,128)(2,1)} %w_o.1, bf16[16,2048]{1,0:T(8,128)(2,1)} %w_u.1, ...), custom_call_target="tpu_custom_call" | custom-call | tf_op jit(solution)/shard_map/pallas_call | solution.py:763
  185.3 0.0 copy-start.1
  185.3 2.2 %convert_element_type.4 = f32[256,1024]{1,0:T(8,128)} convert(bf16[256,1024]{1,0:T(8,128)(2,1)} %get-tuple-element.22) | non-fusion elementwise | flops 262144 | bytes 1572864 | tf_op jit(solution)/shard_map/convert_element_type | solution.py:806
  187.5 0.0 copy-done.1
  187.6 0.0 copy-start
  187.6 0.7 fusion.1
  188.2 0.7 fusion
  189.0 1.3 fusion.3
  190.2 1.3 dynamic_slice.29
  191.5 1.3 fusion.2
  192.8 0.0 copy-done
  192.8 0.8 copy.38
  (2 shorter events, 0.1 us)
Async XLA Ops:
  185.3 2.2 %copy-start.1 = (bf16[24,16,256]{2,1,0:T(8,128)(2,1)S(1)}, bf16[24,16,256]{2,1,0:T(8,128)(2,1)}, u32[]{:S(2)}) copy-start(bf16[24,16,256]{2,1,0:T(8,128)(2,1)} %get-tuple-element.23) | copy-start | bytes 589828
  187.6 5.2 %copy-start = (bf16[256,1024]{1,0:T(8,128)(2,1)S(1)}, bf16[256,1024]{1,0:T(8,128)(2,1)}, u32[]{:S(2)}) copy-start(bf16[256,1024]{1,0:T(8,128)(2,1)} %get-tuple-element.56) | copy-start | bytes 1572868

commit v2 on v1

--- a/solution.py
+++ b/solution.py
@@ -11,9 +11,10 @@
 
 TILES = 24
 COLS = 256
-PHASES, ROUTES, STEPS = 4, 3, 6
+PHASES, ROUTES, STEPS = 4, 3, 4
 VEC_ROWS = 96
 ORDERS = ((2, 0, 1), (1, 2, 0), (0, 1, 2))
+PARTNERS = (1, 3, 2)
 
 
 def position():
@@ -48,56 +49,60 @@
 
 
 class Ring:
-    def __init__(self, sems):
-        self.send, self.recv = sems
+    def __init__(self, buffer, sems, sizes):
+        self.buffer, (self.send, self.recv), self.sizes = buffer, sems, sizes
         self.chip, self.core = position()
 
-    def copy(self, phase, route, step, way, axis, src, dst):
-        sem = ((phase * ROUTES + route) * STEPS + step) * 2 + way
-        target = device(moved(self.chip, axis, 1 if way == 0 else 3), self.core)
+    def copy(self, phase, step, target, src, dst):
+        sem = phase * STEPS + step
         return pltpu.make_async_remote_copy(
             src_ref=src, dst_ref=dst, send_sem=self.send.at[sem], recv_sem=self.recv.at[sem],
             device_id=target, device_id_type=MESH,
         )
 
-    def start(self, phase, route, step):
-        for c in self.copies(phase, route, step):
-            c.start()
-
-    def wait_recv(self, phase, route, step):
-        for c in self.copies(phase, route, step):
-            c.wait_recv()
-
-    def wait_send(self, phase, route, step):
-        for c in self.copies(phase, route, step):
-            c.wait_send()
+    def partner(self, axis, way):
+        return device(moved(self.chip, axis, PARTNERS[way]), self.core)
+
+    def start(self, phase, step):
+        for route in range(ROUTES):
+            for c in self.copies(phase, route, step):
+                c.start()
+
+    def all_of(self, phase, step):
+        tiles, ny, nx, nz = self.sizes[step]
+        whole = self.buffer.at[pl.ds(0, tiles), pl.ds(0, ny), pl.ds(0, nx), pl.ds(0, nz)]
+        return self.copy(phase, step, self.partner(0, 0), whole, whole)
+
+    def wait_recv(self, phase, step):
+        self.all_of(phase, step).wait_recv()
+
+    def wait_send(self, phase, step):
+        self.all_of(phase, step).wait_send()
 
 
 class Gather(Ring):
     def __init__(self, w, sems):
-        super().__init__(sems)
-        self.w = w
+        super().__init__(w, sems, ((18, 1, 1, 1), (18, 1, 1, 4), (12, 1, 4, 4), (6, 1, 4, 4)))
 
     def copies(self, phase, route, step):
-        order = ORDERS[route]
-        axis, full = order[step // 2], order[: step // 2]
+        order, k = ORDERS[route], min(step, 2)
+        axis, full = order[k], order[:k]
         tile = first_tile(phase, route)
         out = []
-        for way in range(2):
-            if step % 2 == 0:
-                part = self.w.at[(pl.ds(tile, 2),) + blocks(self.chip, full)]
+        for way in range(3 if step < 2 else 2):
+            if step < 3:
+                part = self.buffer.at[(pl.ds(tile, 2),) + blocks(self.chip, full)]
             else:
-                behind = moved(self.chip, axis, 3 if way == 0 else 1)
-                part = self.w.at[(pl.ds(tile + way, 1),) + blocks(behind, full)]
-            out.append(self.copy(phase, route, step, way, axis, part, part))
+                behind = moved(self.chip, axis, PARTNERS[1 - way])
+                part = self.buffer.at[(pl.ds(tile + way, 1),) + blocks(behind, full)]
+            out.append(self.copy(phase, step, self.partner(axis, way), part, part))
         return out
 
     def step(self, phase, step):
-        for route in range(ROUTES):
-            if step:
-                self.wait_recv(phase, route, step - 1)
-            if step < STEPS:
-                self.start(phase, route, step)
+        if step:
+            self.wait_recv(phase, step - 1)
+        if step < STEPS:
+            self.start(phase, step)
 
 
 def landing_shapes():
@@ -111,34 +116,33 @@
 
 class Scatter(Ring):
     def __init__(self, g, landings, sems):
-        super().__init__(sems)
+        super().__init__(g, sems, ((6, 1, 4, 4), (12, 1, 4, 4), (18, 1, 1, 4), (18, 1, 1, 1)))
         self.g, self.landings = g, landings
 
     def at(self, route, step):
-        order = ORDERS[route]
-        return order[2 - step // 2], order[: 2 - step // 2]
+        order, k = ORDERS[route], max(step - 1, 0)
+        return order[2 - k], order[: 2 - k]
 
     def landing(self, phase, route, step):
-        return self.landings[(phase * ROUTES + route) * 3 + step // 2]
+        return self.landings[(phase * ROUTES + route) * 3 + max(step - 1, 0)]
 
     def copies(self, phase, route, step):
         axis, full = self.at(route, step)
         tile = first_tile(phase, route)
         landed = self.landing(phase, route, step)
         out = []
-        for way in range(2):
-            if step % 2 == 0:
+        for way in range(2 if step < 2 else 3):
+            if step == 0:
                 src = self.g.at[(pl.ds(tile + way, 1),) + blocks(moved(self.chip, axis, 2), full)]
                 dst = landed.at[pl.ds(way, 1)]
             else:
-                ahead = moved(self.chip, axis, 1 if way == 0 else 3)
+                ahead = moved(self.chip, axis, PARTNERS[way])
                 src = self.g.at[(pl.ds(tile, 2),) + blocks(ahead, full)]
-                dst = landed.at[pl.ds(2 + 2 * way, 2)]
-            out.append(self.copy(phase, route, step, way, axis, src, dst))
+                dst = landed.at[pl.ds(2 * way + (2 if step == 1 else 0), 2)]
+            out.append(self.copy(phase, step, self.partner(axis, way), src, dst))
         return out
 
     def take(self, phase, route, step):
-        self.wait_recv(phase, route, step)
         axis, full = self.at(route, step)
         tile = first_tile(phase, route)
         landed = self.landing(phase, route, step)
@@ -161,17 +165,18 @@
             lax.fori_loop(0, ny, one, 0)
 
         for t in range(2):
-            if step % 2 == 0:
-                add(t, start_of(moved(self.chip, axis, 1 if t == 0 else 3)), (t,))
+            if step == 0:
+                add(t, start_of(moved(self.chip, axis, PARTNERS[t])), (t,))
             else:
-                add(t, start_of(self.chip), (2 + t, 4 + t))
+                add(t, start_of(self.chip), (2 + t, 4 + t) if step == 1 else (t, 2 + t, 4 + t))
 
     def step(self, phase, step):
-        for route in range(ROUTES):
-            if step:
+        if step:
+            self.wait_recv(phase, step - 1)
+            for route in range(ROUTES):
                 self.take(phase, route, step - 1)
-            if step < STEPS:
-                self.start(phase, route, step)
+        if step < STEPS:
+            self.start(phase, step)
 
 
 def greet(others):
@@ -186,39 +191,47 @@
     return device(chip, 1 - core)
 
 
-def vector_partner(stage):
-    chip, core = position()
-    if stage == 0:
-        return device(chip, 1 - core)
-    axis = (stage - 1) // 2
-    c = chip[axis]
-    new = c + 1 - 2 * lax.rem(c, 2) if stage % 2 else 3 - c
-    return device(tuple(new if k == axis else v for k, v in enumerate(chip)), core)
-
-
 class VectorSum:
     def __init__(self, kept, came, sems, base):
         self.kept, self.came, (self.send, self.recv), self.base = kept, came, sems, base
-
-    def copy(self, stage):
+        self.chip, self.core = position()
+
+    def copy(self, stage, target, src, dst):
         return pltpu.make_async_remote_copy(
-            src_ref=self.kept.at[stage],
-            dst_ref=self.came.at[stage],
+            src_ref=src,
+            dst_ref=dst,
             send_sem=self.send.at[self.base + stage],
             recv_sem=self.recv.at[self.base + stage],
-            device_id=vector_partner(stage),
+            device_id=target,
             device_id_type=MESH,
         )
 
+    def targets(self, stage):
+        if stage == 0:
+            return [device(self.chip, 1 - self.core)]
+        return [device(moved(self.chip, stage - 1, by), self.core) for by in PARTNERS]
+
+    def all_of(self, stage):
+        targets = self.targets(stage)
+        whole = self.came.at[pl.ds(max(3 * stage - 2, 0), len(targets))]
+        return self.copy(stage, targets[0], whole, whole)
+
     def step(self, stage):
         if stage:
-            self.copy(stage - 1).wait_recv()
-            self.kept[stage] = self.kept[stage - 1] + self.came[stage - 1]
-        if stage < 7:
-            self.copy(stage).start()
+            self.all_of(stage - 1).wait_recv()
+            own = self.kept[stage - 1]
+            if stage == 1:
+                self.kept[1] = own + self.came[0]
+            else:
+                slot = 3 * stage - 5
+                self.kept[stage] = (own + self.came[slot + 2]) + (self.came[slot] + self.came[slot + 1])
+        if stage < 4:
+            for n, target in enumerate(self.targets(stage)):
+                there = self.came.at[max(3 * stage - 2, 0) + n]
+                self.copy(stage, target, self.kept.at[stage], there).start()
 
     def wait_send(self, stage):
-        self.copy(stage).wait_send()
+        self.all_of(stage).wait_send()
 
 
 GROUP = 512
@@ -255,7 +268,7 @@
     w_q, w_k, w_v, w_o, w_u, w_d,
     v_0, v_1, v_2, v_3, v_4, v_5, v_6, v_7, v_8, segment, tokens, out_grad,
     layer_out, input_grad, shares, vec_out,
-    w, g, x, n1, gd, tr, qkv, probs, bias, ctx, gctx, ds, part, leave, come,
+    w, g, x, n1, gd, tr, x_tr, qkv, probs, bias, ctx, gctx, ds, part, leave, come,
     hat, inv, d_two, cot, act, slope, seg_here, seg_own, segments, segcol, features, biases, bias_sums, sums, out_rows,
     r_0, r_1, r_2, r_3, r_4, r_5, r_6, r_7, r_8, placed,
     kept, came, kept_front, came_front, kept_tail, came_tail,
@@ -305,7 +318,7 @@
             device_id=twin, device_id_type=MESH,
         )
 
-    greet([device(moved(chip, axis, by), core) for axis in range(3) for by in (1, 3)] + [twin, diagonal])
+    greet([device(moved(chip, axis, by), core) for axis in range(3) for by in PARTNERS] + [twin, diagonal])
 
     weight_moves = []
     tile = 0
@@ -313,31 +326,24 @@
         for k in range(count):
             weight_moves.append(
                 (
-                    tile,
+                    tile // 6,
                     ref.at[:, pl.ds(k * COLS, COLS)],
                     w.at[tile, y, x_at, z],
                     w.at[(tile,) + opposite_chip],
                 )
             )
             tile += 1
-    for move in weight_moves[:6]:
-        swap_start(*move)
-    row_move = (TILES, tokens, x.at[own_rows], x.at[other_rows])
-    swap_start(*row_move)
-    for move in weight_moves[6:]:
+    for move in weight_moves:
         swap_start(*move)
 
     gather = Gather(w, (gsend, grecv))
     vectors = VectorSum(kept, came, (vsend, vrecv), 0)
 
     def arrived(phase):
-        for move in weight_moves[6 * phase : 6 * phase + 6]:
-            swap_wait(*move)
-
-    arrived(0)
-    gather.step(0, 0)
-
-    for load in loads:
+        group = w.at[pl.ds(6 * phase, 6), y, x_at, z]
+        swap_wait(phase, group, group, group)
+
+    for load in loads[:-1]:
         load.wait()
     dp, tensor = lax.axis_index("dp"), lax.axis_index("tensor")
     placed[...] = jnp.zeros((VEC_ROWS, 128), F32)
@@ -352,46 +358,39 @@
     kept[0] = placed[...].astype(BF16)
     vectors.step(0)
     seg_own[...] = jnp.broadcast_to(seg_here[...].astype(F32), (8, GROUP))
-    seg_move = (TILES + 1, seg_own, segments, segments)
+    seg_move = (5, seg_own, segments, segments)
     swap_start(*seg_move)
-
+    arrived(0)
+    gather.step(0, 0)
+    row_move = (4, tokens, x.at[own_rows], x.at[other_rows])
+    swap_start(*row_move)
+    vectors.step(1)
+    for phase in (1, 2, 3):
+        arrived(phase)
+        gather.step(phase, 0)
     gather.step(0, 1)
-    vectors.step(1)
-    arrived(1)
-    gather.step(1, 0)
-    swap_wait(*row_move)
-    rows_copy = to_twin(0, x.at[own_rows], x.at[own_rows])
-    rows_copy.start()
-    gather.step(0, 2)
     vectors.step(2)
     gather.step(1, 1)
-    arrived(2)
-    gather.step(2, 0)
-    gather.step(0, 3)
-    vectors.step(3)
-    gather.step(1, 2)
-    gather.step(2, 1)
-    arrived(3)
-    gather.step(0, 4)
-    vectors.step(4)
-    gather.step(1, 3)
-    gather.step(2, 2)
-    gather.step(3, 0)
-    vectors.step(5)
 
     swap_wait(*seg_move)
     across_lanes = jnp.broadcast_to(segments[0:1, :], (128, GROUP))
     segcol[...] = across_lanes.T
     for k in range(4):
         cols = slice(k * 128, k * 128 + 128)
-        bias[:, cols] = jnp.where(segcol[...] == segments[0:1, cols], 0.0, -1000000000.0)
-    vectors.step(6)
-    gather.step(0, 5)
-    gather.step(1, 4)
-    gather.step(2, 3)
+        bias[:, cols] = jnp.where(segcol[...] == segments[0:1, cols], 0.0, -1000000000.0).astype(BF16)
+    gather.step(0, 2)
+    vectors.step(3)
+    gather.step(2, 1)
+    swap_wait(*row_move)
+    rows_copy = to_twin(0, x.at[own_rows], x.at[own_rows])
+    rows_copy.start()
+    loads[-1].wait()
+    out_rows[...] = d_two[...].astype(BF16)
+    gather.step(0, 3)
+    gather.step(1, 2)
     gather.step(3, 1)
-    vectors.step(7)
-    placed[...] = kept[7].astype(F32)
+    vectors.step(4)
+    placed[...] = kept[4].astype(F32)
     for n in range(6):
         for k in range(8):
             features[n, :, k * 128 : k * 128 + 128] = placed[48 + n * 8 + k : 49 + n * 8 + k, :]
@@ -406,8 +405,14 @@
             lanes = slice(half * 128, half * 128 + 128)
             biases[6 + k, :, lanes] = placed[pl.ds(16 + core * 16 + k * 2 + half, 1), :]
     rows_copy.wait_recv()
-    out_rows[...] = d_two[...].astype(BF16)
-    gather.step(0, 6)
+
+    def turn(ref, out=tr):
+        for k in range(4):
+            rows = slice(k * COLS, k * COLS + COLS)
+            out[rows, :] = ref[:, rows].T
+
+    turn(x, x_tr)
+    gather.step(0, 4)
 
     def weight(tile):
         return w[tile].reshape(WIDTH, COLS)
@@ -418,8 +423,8 @@
         qkv[2 * t + 1] = made[:, 128:]
 
     loop(6, project)
-    gather.step(2, 4)
-    gather.step(3, 2)
+    gather.step(1, 3)
+    gather.step(2, 2)
     low_lanes = lax.broadcasted_iota(jnp.int32, (1, PAIR), 1) < HEAD_DIM
 
     def only(head, values):
@@ -432,7 +437,7 @@
             query = qkv[pair, rows]
             outs = []
             for head in range(2):
-                scores = dot(qkv[4 + pair], only(head, query), NT) * SCALE + bias[:, rows]
+                scores = dot(qkv[4 + pair], only(head, query), NT) * SCALE + bias[:, rows].astype(F32)
                 scores = jnp.exp(scores - jnp.max(scores, axis=0, keepdims=True))
                 weights = scores * (1.0 / jnp.sum(scores, axis=0, keepdims=True))
                 weights = weights.astype(BF16)
@@ -441,17 +446,15 @@
             ctx[pair, rows] = jnp.where(low_lanes, outs[0], outs[1]).astype(BF16)
 
     attend(0)
-    gather.step(1, 5)
-    gather.step(2, 5)
+    gather.step(3, 2)
+    attend(1)
+    gather.step(2, 3)
+    attend(2)
     gather.step(3, 3)
-    attend(1)
-    gather.step(3, 4)
-    attend(2)
-    cot_move = (TILES + 2, out_rows, cot, cot)
+    cot_move = (6, out_rows, cot, cot)
     swap_start(*cot_move)
     attend(3)
-    gather.step(1, 6)
-    gather.step(3, 5)
+    gather.step(1, 4)
 
     terms_sent = []
 
@@ -542,9 +545,9 @@
             slope[t, rows] = (below + pre * bell).astype(BF16)
 
     loop(4, up)
-    gather.step(2, 6)
+    gather.step(2, 4)
     loop(4, lambda t: up(t + 4))
-    gather.step(3, 6)
+    gather.step(3, 4)
     row_terms(1, range(DOWN_TILE, TILES), lambda t, rows: act[t, rows])
     swap_wait(*cot_move)
 
@@ -567,28 +570,23 @@
         gd[there] = back.astype(BF16)
 
     by_chunks(second_norm)
-    out_move = (TILES + 3, out_rows, layer_out, layer_out)
+    out_move = (7, out_rows, layer_out, layer_out)
     swap_start(*out_move)
     share_rows(6, gd)
 
-    def turn(ref):
+    def store_grad(tile, right, left=tr):
         for k in range(4):
-            rows = slice(k * COLS, k * COLS + COLS)
-            tr[rows, :] = ref[:, rows].T
-
-    def store_grad(tile, right):
-        for k in range(4):
-            made = dot(tr[k * COLS : k * COLS + COLS, :], right)
+            made = dot(left[k * COLS : k * COLS + COLS, :], right)
             g[tile, k] = made.astype(BF16).reshape(4, 4, 16, COLS)
 
     scatter = Scatter(g, landings, (ssend, srecv))
     share_moves = []
 
     def reduced(phase):
-        scatter.step(phase, 6)
+        scatter.step(phase, 4)
         tiles = pl.ds(6 * phase, 6)
         share_moves.append(
-            (TILES + 5 + phase, g.at[tiles, y, x_at, z], shares.at[tiles], shares.at[tiles])
+            (9 + phase, g.at[tiles, y, x_at, z], shares.at[tiles], shares.at[tiles])
         )
         swap_start(*share_moves[-1])
 
@@ -607,7 +605,6 @@
     loop(4, lambda t: store_grad(UP_TILE + 4 + t, slope[4 + t]))
     scatter.step(2, 0)
     loop(4, lambda t: store_grad(UP_TILE + t, slope[t]))
-    scatter.step(3, 2)
     row_terms(2, range(UP_TILE, DOWN_TILE), lambda t, rows: slope[t, rows])
 
     def first_norm_back(here, there):
@@ -621,13 +618,13 @@
 
     shared.pop(5).wait_send()
     d1 = n1
+    scatter.step(3, 2)
     scatter.step(2, 1)
     by_chunks(first_norm_back)
     share_rows(7, d1)
     turn(d1)
     loop(2, lambda u: store_grad(OUT_TILE + u, side_by_side(ctx, 2 * u)))
     scatter.step(1, 0)
-    scatter.step(2, 2)
     scatter.step(3, 3)
 
     kept_front[0] = jnp.zeros((VEC_ROWS - 16, 128), F32)
@@ -639,7 +636,7 @@
         for k in range(8):
             at = 32 + n * 8 + k
             kept_front[0, at : at + 1, :] = sums[n, :, k * 128 : k * 128 + 128]
-    front = VectorSum(kept_front, came_front, (vsend, vrecv), 7)
+    front = VectorSum(kept_front, came_front, (vsend, vrecv), 4)
     front.step(0)
 
     def context_back(u):
@@ -648,8 +645,7 @@
         gctx[2 * u + 1] = made[:, 128:]
 
     loop(2, context_back)
-    scatter.step(1, 1)
-    scatter.step(3, 4)
+    scatter.step(2, 2)
     front.step(1)
 
     def attend_back(pair):
@@ -669,69 +665,55 @@
             bias_sums[14 + at + pair, :, :PAIR] = jnp.sum(made.astype(F32), axis=0, keepdims=True)
 
     attend_back(0)
-    scatter.step(2, 3)
-    scatter.step(1, 2)
-    scatter.step(3, 5)
+    scatter.step(1, 1)
+    reduced(3)
     front.step(2)
     attend_back(1)
-    scatter.step(2, 4)
-    scatter.step(1, 3)
-    reduced(3)
+    scatter.step(2, 3)
     front.step(3)
     attend_back(2)
-    scatter.step(2, 5)
-    scatter.step(1, 4)
+    scatter.step(1, 2)
     front.step(4)
+    reduced(2)
     attend_back(3)
+    scatter.step(1, 3)
     kept_tail[0] = jnp.zeros((16, 128), F32)
     for k in range(4):
         kept_tail[0, pl.ds(core * 4 + k, 1), :] = bias_sums[14 + k, :, :PAIR]
         kept_tail[0, pl.ds(8 + core * 4 + k, 1), :] = bias_sums[22 + k, :, :PAIR]
-    tail = VectorSum(kept_tail, came_tail, (vsend, vrecv), 14)
+    tail = VectorSum(kept_tail, came_tail, (vsend, vrecv), 8)
     tail.step(0)
-    turn(x)
-    loop(6, lambda t: store_grad(t, side_by_side(qkv, 2 * t)))
+    loop(6, lambda t: store_grad(t, side_by_side(qkv, 2 * t), x_tr))
     scatter.step(0, 0)
-    scatter.step(1, 5)
-    reduced(2)
     tail.step(1)
-    front.step(5)
+    reduced(1)
     row_terms(3, range(6), lambda t, rows: side_by_side(qkv, 2 * t, rows))
     scatter.step(0, 1)
     tail.step(2)
-    front.step(6)
 
     def last_rows(here, there):
         cot[here] = (d_two[here] + part[here] + come[here].astype(F32)).astype(BF16)
 
     by_chunks(last_rows)
-    grad_move = (TILES + 4, cot, input_grad, input_grad)
+    grad_move = (8, cot, input_grad, input_grad)
     swap_start(*grad_move)
     scatter.step(0, 2)
     tail.step(3)
-    front.step(7)
-    reduced(1)
     scatter.step(0, 3)
     tail.step(4)
-    scatter.step(0, 4)
-    tail.step(5)
-    scatter.step(0, 5)
-    tail.step(6)
     reduced(0)
-    tail.step(7)
-    vec_out[0:16] = kept_tail[7]
-    vec_out[16:] = kept_front[7]
+    vec_out[0:16] = kept_tail[4]
+    vec_out[16:] = kept_front[4]
 
     for move in [out_move, grad_move] + share_moves:
         swap_wait(*move)
     for copy in sent + terms_sent[-1:] + list(shared.values()):
         copy.wait_send()
     for phase in range(PHASES):
-        for route in range(ROUTES):
-            for step in range(STEPS):
-                gather.wait_send(phase, route, step)
-                scatter.wait_send(phase, route, step)
-    for stage in range(7):
+        for step in range(STEPS):
+            gather.wait_send(phase, step)
+            scatter.wait_send(phase, step)
+    for stage in range(4):
         vectors.wait_send(stage)
         front.wait_send(stage)
         tail.wait_send(stage)
@@ -744,8 +726,8 @@
     front = VEC_ROWS - 16
     scratch = [
         (full, BF16), (full, BF16),
-        (rows, BF16), (rows, BF16), (rows, BF16), ((WIDTH, GROUP), BF16),
-        ((12, GROUP, PAIR), BF16), ((8, GROUP, GROUP), BF16), ((GROUP, GROUP), F32),
+        (rows, BF16), (rows, BF16), (rows, BF16), ((WIDTH, GROUP), BF16), ((WIDTH, GROUP), BF16),
+        ((12, GROUP, PAIR), BF16), ((8, GROUP, GROUP), BF16), ((GROUP, GROUP), BF16),
         ((4, GROUP, PAIR), BF16), ((4, GROUP, PAIR), BF16), ((2, GROUP, GROUP), BF16),
         (half, F32), (half, BF16), (half, BF16),
         (half, F32), ((HALF, 128), F32), (half, F32), (half, BF16),
@@ -755,11 +737,11 @@
         (half, BF16),
     ] + [((length,), BF16) for length in VECTORS] + [
         ((VEC_ROWS, 128), F32),
-        ((8, VEC_ROWS, 128), BF16), ((7, VEC_ROWS, 128), BF16),
-        ((8, front, 128), F32), ((7, front, 128), F32),
-        ((8, 16, 128), F32), ((7, 16, 128), F32),
+        ((5, VEC_ROWS, 128), BF16), ((10, VEC_ROWS, 128), BF16),
+        ((5, front, 128), F32), ((10, front, 128), F32),
+        ((5, 16, 128), F32), ((10, 16, 128), F32),
     ]
-    sems = [PHASES * ROUTES * STEPS * 2] * 4 + [21] * 2 + [TILES + 9] * 2 + [8] * 2 + [11]
+    sems = [PHASES * STEPS] * 4 + [12] * 2 + [13] * 2 + [8] * 2 + [11]
     return pl.pallas_call(
         layer_kernel,
         out_shape=(
@@ -779,34 +761,75 @@
     )(*arrays)
 
 
-def unpacked_vectors(flat):
-    dp, low = lax.axis_index("dp"), lax.axis_index("tensor")
-    out, at = [], 0
-    for length in (8, 8, 32):
-        out.append(lax.dynamic_slice(flat, (at + (low * 64 + dp) * length,), (length,)))
-        at += length * 128
-    for _ in range(6):
-        out.append(lax.dynamic_slice(flat, (at + dp * 16,), (16,)))
-        at += 1024
-    return out
+def finish_kernel(
+    layer_in, grad_in, shares_in, totals_in,
+    layer_out, input_grad, g_q, g_k, g_v, g_o, g_u, g_d, o_0, o_1, o_2, o_3, o_4, o_5, o_6, o_7, o_8,
+    layer, grad_low, shares, totals, grad, f_q, f_k, f_v, f_o, f_u, f_d, s_0, s_1, s_2, s_3, s_4, s_5, s_6, s_7, s_8,
+    in_sem, out_sem,
+):
+    pairs = ((totals_in, totals), (shares_in, shares), (grad_in, grad_low), (layer_in, layer))
+    loads = [pltpu.make_async_copy(src, dst, in_sem.at[n]) for n, (src, dst) in enumerate(pairs)]
+    for load in loads:
+        load.start()
+    dp, tensor = lax.axis_index("dp"), lax.axis_index("tensor")
+    stores = []
+
+    def store(src, dst):
+        stores.append(pltpu.make_async_copy(src, dst, out_sem.at[len(stores)]))
+        stores[-1].start()
+
+    loads[0].wait()
+    rows = (s_0, s_1, s_2, s_3, s_4, s_5, s_6, s_7, s_8)
+    outs = (o_0, o_1, o_2, o_3, o_4, o_5, o_6, o_7, o_8)
+    for n, (kept, out, length, row) in enumerate(zip(rows, outs, VECTORS, VECTOR_ROWS)):
+        at = (tensor * 64 + dp if n < 3 else dp) * length
+        value = jnp.broadcast_to(totals[pl.ds(row + at // 128, 1), :], (8, 128))
+        value = pltpu.roll(value, lax.rem(128 - lax.rem(at, 128), 128), 1)
+        kept[...] = value[0:1, :length].reshape(length)
+        store(kept, out)
+    loads[1].wait()
+    tile = 0
+    for kept, out, count in zip((f_q, f_k, f_v, f_o, f_u, f_d), (g_q, g_k, g_v, g_o, g_u, g_d), WEIGHT_TILES):
+        for k in range(count):
+            kept[:, k * COLS : k * COLS + COLS] = shares[tile].astype(F32)
+            tile += 1
+        store(kept, out)
+    loads[2].wait()
+    for k in range(4):
+        part = slice(k * 64, k * 64 + 64)
+        grad[part] = grad_low[part].astype(F32)
+        store(grad.at[part], input_grad.at[part])
+    loads[3].wait()
+    store(layer, layer_out)
+    for copy in stores:
+        copy.wait()
+
+
+def finish_call(*arrays):
+    half = (HALF, WIDTH)
+    shares = [(16, count * COLS) for count in WEIGHT_TILES]
+    vectors = [(length,) for length in VECTORS]
+    outs = [(half, BF16)] + [(shape, F32) for shape in [half] + shares + vectors]
+    scratch = [(half, BF16), (half, BF16), ((TILES, 16, COLS), BF16), ((VEC_ROWS, 128), F32)] + outs[1:]
+    return pl.pallas_call(
+        finish_kernel,
+        out_shape=tuple(jax.ShapeDtypeStruct(*o) for o in outs),
+        in_specs=[pl.BlockSpec(memory_space=pl.ANY)] * len(arrays),
+        out_specs=(pl.BlockSpec(memory_space=pl.ANY),) * len(outs),
+        scratch_shapes=[pltpu.VMEM(*o) for o in scratch]
+        + [pltpu.SemaphoreType.DMA((4,)), pltpu.SemaphoreType.DMA((20,))],
+    )(*arrays)
 
 
 def on_device(
     tokens, segment, w_query, w_key, w_value, w_out, w_up, w_down, b_query, b_value, b_up,
     b_out, b_down, gain_one, shift_one, gain_two, shift_two, out_grad,
 ):
-    layer_out, input_grad, shares, totals = layer_call(
+    made = layer_call(
         w_query, w_key, w_value, w_out, w_up, w_down, b_query, b_value, b_up,
         b_out, b_down, gain_one, shift_one, gain_two, shift_two, segment, tokens, out_grad,
     )
-    shares = shares.astype(F32).transpose(1, 0, 2).reshape(16, TILES * COLS)
-    ends = [sum(WEIGHT_TILES[:k]) * COLS for k in range(1, 6)]
-    return (
-        layer_out,
-        input_grad.astype(F32),
-        *jnp.split(shares, ends, axis=1),
-        *unpacked_vectors(totals.reshape(-1)),
-    )
+    return tuple(finish_call(*made))
 
 
 def solution(mesh):

time: 194 us -> 170 us (0.88)
  Pallas kernels: 185 us -> 169 us
  local copies, waits for them, and re-layouts: 6.03 us -> 0 us
  other arithmetic: 2.2 us -> 0 us
    pallas_call x1, Pallas kernels: 185 us -> 166 us  [layer_call(): pl.pallas_call(layer_kernel, out_shape=(jax.ShapeDtypeStruct(half, BF16),...]
    dynamic_slice x3 -> x0, local copies, waits for them, and re-layouts: 3.84 us -> none  [the longest x2 2.53 us: unpacked_vectors(): lax.dynamic_slice(flat, (at + (low * 64 + dp) * length,), (length,))]
    pallas_call x0 -> x1, Pallas kernels: none -> 2.55 us  [finish_call(): pl.pallas_call(finish_kernel, out_shape=tuple((jax.ShapeDtypeStruct(*o) f...]
    convert_element_type x1 -> x0, other arithmetic: 2.17 us -> none  [on_device(): input_grad.astype(F32)]
where the time goes in v2:
time: 170 us
  Pallas kernels  169 us (99%)
    pallas_call x1, Pallas kernels, layer_call(): pl.pallas_call(layer_kernel, out_shape=(jax.ShapeDtypeStruct(half, BF16),...  166 us

profile of v2, /device:TPU:1, one launch (start us, length us, event | category | flops | bytes accessed | tf_op | source)
XLA Modules:
  0.0 169.8 jit_solution(12356832233457445200)
XLA Ops:
  0.7 166.4 %shard_map.305 = (bf16[256,1024]{1,0:T(8,128)(2,1)}, bf16[256,1024]{1,0:T(8,128)(2,1)}, bf16[24,16,256]{2,1,0:T(8,128)(2,1)}, f32[96,128]{1,0:T(8,128)}) custom-call(bf16[16,512]{1,0:T(8,128)(2,1)} %w_q.1, bf16[16,512]{1,0:T(8,128)(2,1)} %w_k.1, bf16[16,512]{1,0:T(8,128)(2,1)} %w_v.1, bf16[16,512]{1,0:T(8,128)(2,1)} %w_o.1, bf16[16,2048]{1,0:T(8,128)(2,1)} %w_u.1, ...), custom_call_target="tpu_custom_call" | custom-call | tf_op jit(solution)/shard_map/pallas_call | solution.py:745
  167.1 2.5 %shard_map.306 = (bf16[256,1024]{1,0:T(8,128)(2,1)}, f32[256,1024]{1,0:T(8,128)}, f32[16,512]{1,0:T(8,128)}, f32[16,512]{1,0:T(8,128)}, f32[16,512]{1,0:T(8,128)...) custom-call(bf16[256,1024]{1,0:T(8,128)(2,1)} %get-tuple-element.21., ...), custom_call_target="tpu_custom_call" | custom-call | tf_op jit(solution)/shard_map/pallas_call | solution.py:814

commit v3 on v2

--- a/solution.py
+++ b/solution.py
@@ -49,8 +49,8 @@
 
 
 class Ring:
-    def __init__(self, buffer, sems, sizes):
-        self.buffer, (self.send, self.recv), self.sizes = buffer, sems, sizes
+    def __init__(self, buffer, sems):
+        self.buffer, (self.send, self.recv) = buffer, sems
         self.chip, self.core = position()
 
     def copy(self, phase, step, target, src, dst):
@@ -63,13 +63,16 @@
     def partner(self, axis, way):
         return device(moved(self.chip, axis, PARTNERS[way]), self.core)
 
+    def start_route(self, phase, route, step):
+        for c in self.copies(phase, route, step):
+            c.start()
+
     def start(self, phase, step):
         for route in range(ROUTES):
-            for c in self.copies(phase, route, step):
-                c.start()
+            self.start_route(phase, route, step)
 
     def all_of(self, phase, step):
-        tiles, ny, nx, nz = self.sizes[step]
+        tiles, ny, nx, nz = self.size(phase, step)
         whole = self.buffer.at[pl.ds(0, tiles), pl.ds(0, ny), pl.ds(0, nx), pl.ds(0, nz)]
         return self.copy(phase, step, self.partner(0, 0), whole, whole)
 
@@ -81,8 +84,8 @@
 
 
 class Gather(Ring):
-    def __init__(self, w, sems):
-        super().__init__(w, sems, ((18, 1, 1, 1), (18, 1, 1, 4), (12, 1, 4, 4), (6, 1, 4, 4)))
+    def size(self, phase, step):
+        return ((18, 1, 1, 1), (18, 1, 1, 4), (12, 1, 4, 4), (6, 1, 4, 4))[step]
 
     def copies(self, phase, route, step):
         order, k = ORDERS[route], min(step, 2)
@@ -105,47 +108,61 @@
             self.start(phase, step)
 
 
+HALVES = (0, 4)
+
+
+def scatter_tiles(phase, route):
+    if phase in HALVES:
+        return 2 * route + HALVES.index(phase), 1
+    return first_tile(phase, route), 2
+
+
+def scatter_steps(phase):
+    return 3 if phase in HALVES else STEPS
+
+
 def landing_shapes():
     shapes = []
-    for _ in range(PHASES):
+    for phase in range(PHASES + 1):
         for order in ORDERS:
             for k in range(3):
-                shapes.append((6,) + block_shape(order[: 2 - k]) + (16, COLS))
+                tiles = 3 if phase in HALVES else 6
+                shapes.append((tiles,) + block_shape(order[: 2 - k]) + (16, COLS))
     return shapes
 
 
 class Scatter(Ring):
     def __init__(self, g, landings, sems):
-        super().__init__(g, sems, ((6, 1, 4, 4), (12, 1, 4, 4), (18, 1, 1, 4), (18, 1, 1, 1)))
+        super().__init__(g, sems)
         self.g, self.landings = g, landings
 
-    def at(self, route, step):
-        order, k = ORDERS[route], max(step - 1, 0)
-        return order[2 - k], order[: 2 - k]
-
-    def landing(self, phase, route, step):
-        return self.landings[(phase * ROUTES + route) * 3 + max(step - 1, 0)]
+    def size(self, phase, step):
+        if phase in HALVES:
+            return ((9, 1, 4, 4), (9, 1, 1, 4), (9, 1, 1, 1))[step]
+        return ((6, 1, 4, 4), (12, 1, 4, 4), (18, 1, 1, 4), (18, 1, 1, 1))[step]
+
+    def at(self, phase, route, step):
+        order, k = ORDERS[route], step if phase in HALVES else max(step - 1, 0)
+        return order[2 - k], order[: 2 - k], self.landings[(phase * ROUTES + route) * 3 + k]
 
     def copies(self, phase, route, step):
-        axis, full = self.at(route, step)
-        tile = first_tile(phase, route)
-        landed = self.landing(phase, route, step)
+        axis, full, landed = self.at(phase, route, step)
+        tile, count = scatter_tiles(phase, route)
         out = []
-        for way in range(2 if step < 2 else 3):
-            if step == 0:
+        for way in range(2 if count == 2 and step < 2 else 3):
+            if count == 2 and step == 0:
                 src = self.g.at[(pl.ds(tile + way, 1),) + blocks(moved(self.chip, axis, 2), full)]
                 dst = landed.at[pl.ds(way, 1)]
             else:
                 ahead = moved(self.chip, axis, PARTNERS[way])
-                src = self.g.at[(pl.ds(tile, 2),) + blocks(ahead, full)]
-                dst = landed.at[pl.ds(2 * way + (2 if step == 1 else 0), 2)]
+                src = self.g.at[(pl.ds(tile, count),) + blocks(ahead, full)]
+                dst = landed.at[pl.ds(count * way + (2 if count == 2 and step == 1 else 0), count)]
             out.append(self.copy(phase, step, self.partner(axis, way), src, dst))
         return out
 
     def take(self, phase, route, step):
-        axis, full = self.at(route, step)
-        tile = first_tile(phase, route)
-        landed = self.landing(phase, route, step)
+        axis, full, landed = self.at(phase, route, step)
+        tile, count = scatter_tiles(phase, route)
         ny, nx, nz = block_shape(full)
 
         def start_of(chip):
@@ -164,18 +181,20 @@
 
             lax.fori_loop(0, ny, one, 0)
 
-        for t in range(2):
-            if step == 0:
+        for t in range(count):
+            if count == 2 and step == 0:
                 add(t, start_of(moved(self.chip, axis, PARTNERS[t])), (t,))
+            elif count == 2 and step == 1:
+                add(t, start_of(self.chip), (2 + t, 4 + t))
             else:
-                add(t, start_of(self.chip), (2 + t, 4 + t) if step == 1 else (t, 2 + t, 4 + t))
+                add(t, start_of(self.chip), (t, count + t, 2 * count + t))
 
     def step(self, phase, step):
         if step:
             self.wait_recv(phase, step - 1)
             for route in range(ROUTES):
                 self.take(phase, route, step - 1)
-        if step < STEPS:
+        if step < scatter_steps(phase):
             self.start(phase, step)
 
 
@@ -252,12 +271,13 @@
     return lax.dot_general(a, b, dims, preferred_element_type=F32)
 
 
-def loop(count, body):
+def loop(count, body, together=2):
     def step(i, carry):
-        body(i)
+        for k in range(together):
+            body(i * together + k)
         return carry
 
-    lax.fori_loop(0, count, step, 0)
+    lax.fori_loop(0, count // together, step, 0)
 
 
 VECTORS = (8, 8, 32, 16, 16, 16, 16, 16, 16)
@@ -371,6 +391,9 @@
     gather.step(0, 1)
     vectors.step(2)
     gather.step(1, 1)
+    gather.step(0, 2)
+    vectors.step(3)
+    gather.step(2, 1)
 
     swap_wait(*seg_move)
     across_lanes = jnp.broadcast_to(segments[0:1, :], (128, GROUP))
@@ -378,18 +401,16 @@
     for k in range(4):
         cols = slice(k * 128, k * 128 + 128)
         bias[:, cols] = jnp.where(segcol[...] == segments[0:1, cols], 0.0, -1000000000.0).astype(BF16)
-    gather.step(0, 2)
-    vectors.step(3)
-    gather.step(2, 1)
     swap_wait(*row_move)
     rows_copy = to_twin(0, x.at[own_rows], x.at[own_rows])
     rows_copy.start()
+    gather.step(0, 3)
+    gather.step(3, 1)
+    gather.step(1, 2)
+    vectors.step(4)
+    gather.step(2, 2)
     loads[-1].wait()
     out_rows[...] = d_two[...].astype(BF16)
-    gather.step(0, 3)
-    gather.step(1, 2)
-    gather.step(3, 1)
-    vectors.step(4)
     placed[...] = kept[4].astype(F32)
     for n in range(6):
         for k in range(8):
@@ -411,6 +432,12 @@
             rows = slice(k * COLS, k * COLS + COLS)
             out[rows, :] = ref[:, rows].T
 
+    def turn_half(ref, half):
+        lanes = pl.ds(pl.multiple_of(half * HALF, HALF), HALF)
+        for k in range(4):
+            rows = slice(k * COLS, k * COLS + COLS)
+            tr[rows, lanes] = ref[lanes, rows].T
+
     turn(x, x_tr)
     gather.step(0, 4)
 
@@ -423,8 +450,6 @@
         qkv[2 * t + 1] = made[:, 128:]
 
     loop(6, project)
-    gather.step(1, 3)
-    gather.step(2, 2)
     low_lanes = lax.broadcasted_iota(jnp.int32, (1, PAIR), 1) < HEAD_DIM
 
     def only(head, values):
@@ -446,14 +471,12 @@
             ctx[pair, rows] = jnp.where(low_lanes, outs[0], outs[1]).astype(BF16)
 
     attend(0)
+    attend(1)
+    gather.step(1, 3)
     gather.step(3, 2)
-    attend(1)
+    attend(2)
+    attend(3)
     gather.step(2, 3)
-    attend(2)
-    gather.step(3, 3)
-    cot_move = (6, out_rows, cot, cot)
-    swap_start(*cot_move)
-    attend(3)
     gather.step(1, 4)
 
     terms_sent = []
@@ -498,7 +521,7 @@
             at = pl.multiple_of(i * chunk, chunk)
             body(pl.ds(at, chunk), pl.ds(pl.multiple_of(core * HALF + at, chunk), chunk))
 
-        loop(HALF // chunk, one)
+        loop(HALF // chunk, one, 1)
 
     def mean(values):
         return jnp.mean(values, axis=-1, keepdims=True)
@@ -524,13 +547,18 @@
         n1[there] = (value * features[gain_one] + features[shift_one]).astype(BF16)
 
     by_chunks(first_norm)
+    gather.step(3, 3)
+    cot_move = (6, out_rows, cot, cot)
+    swap_start(*cot_move)
 
     shared = {}
 
-    def share_rows(n, ref):
+    def share_rows(n, ref, meanwhile=None):
         copy = to_twin(n, ref.at[own_rows], ref.at[own_rows])
         copy.start()
         shared[n] = copy
+        if meanwhile:
+            meanwhile()
         copy.wait_recv()
 
     share_rows(5, n1)
@@ -572,7 +600,8 @@
     by_chunks(second_norm)
     out_move = (7, out_rows, layer_out, layer_out)
     swap_start(*out_move)
-    share_rows(6, gd)
+    share_rows(6, gd, lambda: turn_half(gd, core))
+    turn_half(gd, 1 - core)
 
     def store_grad(tile, right, left=tr):
         for k in range(4):
@@ -583,16 +612,24 @@
     share_moves = []
 
     def reduced(phase):
-        scatter.step(phase, 4)
-        tiles = pl.ds(6 * phase, 6)
-        share_moves.append(
-            (9 + phase, g.at[tiles, y, x_at, z], shares.at[tiles], shares.at[tiles])
-        )
-        swap_start(*share_moves[-1])
-
-    turn(gd)
-    loop(8, lambda t: store_grad(DOWN_TILE + t, act[t]))
-    scatter.step(3, 0)
+        scatter.step(phase, scatter_steps(phase))
+        n = 9 + phase
+        if phase in HALVES:
+            moves = [scatter_tiles(phase, route)[0] for route in range(ROUTES)]
+            whole = pl.ds(0, ROUTES)
+        else:
+            moves = [pl.ds(6 * phase, 6)]
+            whole = moves[0]
+        for tiles in moves:
+            swap_start(n, g.at[tiles, y, x_at, z], shares.at[tiles], shares.at[tiles])
+        share_moves.append((n, g.at[whole, y, x_at, z], shares.at[whole], shares.at[whole]))
+
+    for route in range(ROUTES):
+        for t in (2 + 2 * route, 3 + 2 * route):
+            store_grad(DOWN_TILE + t, act[t])
+        scatter.start_route(3, route, 0)
+    for t in range(2):
+        store_grad(DOWN_TILE + t, act[t])
 
     def up_back(t):
         made = (dot(gd[...], weight(DOWN_TILE + t)) * slope[t].astype(F32)).astype(BF16)
@@ -619,10 +656,13 @@
     shared.pop(5).wait_send()
     d1 = n1
     scatter.step(3, 2)
-    scatter.step(2, 1)
     by_chunks(first_norm_back)
-    share_rows(7, d1)
-    turn(d1)
+    def meanwhile():
+        turn_half(d1, core)
+        scatter.step(2, 1)
+
+    share_rows(7, d1, meanwhile)
+    turn_half(d1, 1 - core)
     loop(2, lambda u: store_grad(OUT_TILE + u, side_by_side(ctx, 2 * u)))
     scatter.step(1, 0)
     scatter.step(3, 3)
@@ -645,8 +685,6 @@
         gctx[2 * u + 1] = made[:, 128:]
 
     loop(2, context_back)
-    scatter.step(2, 2)
-    front.step(1)
 
     def attend_back(pair):
         for half in range(2):
@@ -664,32 +702,40 @@
             qkv[at + pair] = made
             bias_sums[14 + at + pair, :, :PAIR] = jnp.sum(made.astype(F32), axis=0, keepdims=True)
 
+    def store_qkv_grads(half):
+        loop(3, lambda t: store_grad(2 * t + half, side_by_side(qkv, 4 * t + 2 * half), x_tr), 1)
+
     attend_back(0)
+    scatter.step(2, 2)
+    front.step(1)
+    attend_back(1)
     scatter.step(1, 1)
+    store_qkv_grads(0)
+    scatter.step(0, 0)
     reduced(3)
     front.step(2)
-    attend_back(1)
+    attend_back(2)
     scatter.step(2, 3)
     front.step(3)
-    attend_back(2)
+    attend_back(3)
     scatter.step(1, 2)
     front.step(4)
     reduced(2)
-    attend_back(3)
-    scatter.step(1, 3)
     kept_tail[0] = jnp.zeros((16, 128), F32)
     for k in range(4):
         kept_tail[0, pl.ds(core * 4 + k, 1), :] = bias_sums[14 + k, :, :PAIR]
         kept_tail[0, pl.ds(8 + core * 4 + k, 1), :] = bias_sums[22 + k, :, :PAIR]
     tail = VectorSum(kept_tail, came_tail, (vsend, vrecv), 8)
     tail.step(0)
-    loop(6, lambda t: store_grad(t, side_by_side(qkv, 2 * t), x_tr))
-    scatter.step(0, 0)
+    store_qkv_grads(1)
+    scatter.step(4, 0)
+    scatter.step(0, 1)
     tail.step(1)
-    reduced(1)
+    scatter.step(1, 3)
     row_terms(3, range(6), lambda t, rows: side_by_side(qkv, 2 * t, rows))
-    scatter.step(0, 1)
+    scatter.step(0, 2)
     tail.step(2)
+    scatter.step(4, 1)
 
     def last_rows(here, there):
         cot[here] = (d_two[here] + part[here] + come[here].astype(F32)).astype(BF16)
@@ -697,11 +743,12 @@
     by_chunks(last_rows)
     grad_move = (8, cot, input_grad, input_grad)
     swap_start(*grad_move)
-    scatter.step(0, 2)
+    reduced(1)
+    reduced(0)
     tail.step(3)
-    scatter.step(0, 3)
+    scatter.step(4, 2)
     tail.step(4)
-    reduced(0)
+    reduced(4)
     vec_out[0:16] = kept_tail[4]
     vec_out[16:] = kept_front[4]
 
@@ -712,6 +759,8 @@
     for phase in range(PHASES):
         for step in range(STEPS):
             gather.wait_send(phase, step)
+    for phase in range(PHASES + 1):
+        for step in range(scatter_steps(phase)):
             scatter.wait_send(phase, step)
     for stage in range(4):
         vectors.wait_send(stage)
@@ -741,7 +790,7 @@
         ((5, front, 128), F32), ((10, front, 128), F32),
         ((5, 16, 128), F32), ((10, 16, 128), F32),
     ]
-    sems = [PHASES * STEPS] * 4 + [12] * 2 + [13] * 2 + [8] * 2 + [11]
+    sems = [PHASES * STEPS] * 2 + [(PHASES + 1) * STEPS] * 2 + [12] * 2 + [14] * 2 + [8] * 2 + [11]
     return pl.pallas_call(
         layer_kernel,
         out_shape=(

time: 170 us -> 159 us (0.935)
  Pallas kernels: 169 us -> 158 us
    pallas_call x1, Pallas kernels: 166 us -> 155 us  [layer_call(): pl.pallas_call(layer_kernel, out_shape=(jax.ShapeDtypeStruct(half, BF16),...]
where the time goes in v3:
time: 159 us; the launch traced here: 158 us
  Pallas kernels  158 us (99%)
    pallas_call x1, Pallas kernels, layer_call(): pl.pallas_call(layer_kernel, out_shape=(jax.ShapeDtypeStruct(half, BF16),...  155 us

profile of v3, /device:TPU:1, one launch (start us, length us, event | category | flops | bytes accessed | tf_op | source)
XLA Modules:
  0.0 158.5 jit_solution(3463199300310252743)
XLA Ops:
  0.7 155.1 %shard_map.305 = (bf16[256,1024]{1,0:T(8,128)(2,1)}, bf16[256,1024]{1,0:T(8,128)(2,1)}, bf16[24,16,256]{2,1,0:T(8,128)(2,1)}, f32[96,128]{1,0:T(8,128)}) custom-call(bf16[16,512]{1,0:T(8,128)(2,1)} %w_q.1, bf16[16,512]{1,0:T(8,128)(2,1)} %w_k.1, bf16[16,512]{1,0:T(8,128)(2,1)} %w_v.1, bf16[16,512]{1,0:T(8,128)(2,1)} %w_o.1, bf16[16,2048]{1,0:T(8,128)(2,1)} %w_u.1, ...), custom_call_target="tpu_custom_call" | custom-call | tf_op jit(solution)/shard_map/pallas_call | solution.py:794
  155.7 2.5 %shard_map.306 = (bf16[256,1024]{1,0:T(8,128)(2,1)}, f32[256,1024]{1,0:T(8,128)}, f32[16,512]{1,0:T(8,128)}, f32[16,512]{1,0:T(8,128)}, f32[16,512]{1,0:T(8,128)...) custom-call(bf16[256,1024]{1,0:T(8,128)(2,1)} %get-tuple-element.21., ...), custom_call_target="tpu_custom_call" | custom-call | tf_op jit(solution)/shard_map/pallas_call | solution.py:863

commit v4 on v3

--- a/solution.py
+++ b/solution.py
@@ -514,7 +514,7 @@
 
     sent = [rows_copy]
     row_terms(0, range(OUT_TILE, UP_TILE), lambda t, rows: side_by_side(ctx, 2 * t, rows))
-    chunk = 64
+    chunk = 128
 
     def by_chunks(body):
         def one(i):
@@ -742,11 +742,11 @@
 
     by_chunks(last_rows)
     grad_move = (8, cot, input_grad, input_grad)
-    swap_start(*grad_move)
     reduced(1)
     reduced(0)
     tail.step(3)
     scatter.step(4, 2)
+    swap_start(*grad_move)
     tail.step(4)
     reduced(4)
     vec_out[0:16] = kept_tail[4]

time: 159 us -> 158 us (level)
  no operation moved by 1% of the time
where the time goes in v4:
time: 158 us
  Pallas kernels  157 us (99%)
    pallas_call x1, Pallas kernels, layer_call(): pl.pallas_call(layer_kernel, out_shape=(jax.ShapeDtypeStruct(half, BF16),...  154 us

profile of v4, /device:TPU:1, one launch (start us, length us, event | category | flops | bytes accessed | tf_op | source)
XLA Modules:
  0.0 157.6 jit_solution(4833758187485359591)
XLA Ops:
  0.7 154.2 %shard_map.305 = (bf16[256,1024]{1,0:T(8,128)(2,1)}, bf16[256,1024]{1,0:T(8,128)(2,1)}, bf16[24,16,256]{2,1,0:T(8,128)(2,1)}, f32[96,128]{1,0:T(8,128)}) custom-call(bf16[16,512]{1,0:T(8,128)(2,1)} %w_q.1, bf16[16,512]{1,0:T(8,128)(2,1)} %w_k.1, bf16[16,512]{1,0:T(8,128)(2,1)} %w_v.1, bf16[16,512]{1,0:T(8,128)(2,1)} %w_o.1, bf16[16,2048]{1,0:T(8,128)(2,1)} %w_u.1, ...), custom_call_target="tpu_custom_call" | custom-call | tf_op jit(solution)/shard_map/pallas_call | solution.py:794
  154.9 2.5 %shard_map.306 = (bf16[256,1024]{1,0:T(8,128)(2,1)}, f32[256,1024]{1,0:T(8,128)}, f32[16,512]{1,0:T(8,128)}, f32[16,512]{1,0:T(8,128)}, f32[16,512]{1,0:T(8,128)...) custom-call(bf16[256,1024]{1,0:T(8,128)(2,1)} %get-tuple-element.21., ...), custom_call_target="tpu_custom_call" | custom-call | tf_op jit(solution)/shard_map/pallas_call | solution.py:863
